TPU v7x, 128 devices: a whole 4x4x4 slice. The times are simulated.
128 devices in a mesh: dp: 4 (over x_lo, core), fsdp: 32 (over z, y, x_hi).
Axes of the slice: x: 4 (x_hi: 2, x_lo: 2; x = x_hi * 2 + x_lo), y: 4, z: 4, core: 2. Of those that a mesh axis runs over, the one named last changes fastest.
Arguments:
- partials: bfloat16 [4, 256, 512, 512], P('dp', None, 'fsdp'), may hold values from -2 to 2
- stats_left: float32 [256, 512, 512], P(('dp', 'fsdp')), as said below
- stats_right: float32 [256, 512, 512], P(('dp', 'fsdp')), as said below
- root_left: bfloat16 [256, 512, 512], P(('dp', 'fsdp')), as said below
- root_right: bfloat16 [256, 512, 512], P(('dp', 'fsdp')), as said below
- moment: float32 [256, 512, 512], P(('dp', 'fsdp')), may hold values from -3 to 3
- second: float32 [256, 512, 512], P(('dp', 'fsdp')), may hold values from 0.02 to 1
Outputs:
- stats_left_out: float32 [256, 512, 512], P(('dp', 'fsdp'))
- stats_right_out: float32 [256, 512, 512], P(('dp', 'fsdp'))
- moment_out: float32 [256, 512, 512], P(('dp', 'fsdp'))
- second_out: float32 [256, 512, 512], P(('dp', 'fsdp'))
- step_out: float32 [256, 512, 512], P('dp', 'fsdp')
Inputs may be any that keep to these rules, and one draw needn't show every extreme that they name: `stats_left`: each block is symmetric. `stats_right`: each block is symmetric. `root_left`: each block is symmetric. `root_right`: each block is symmetric.
All inputs are finite; a program needn't handle non-finite values.
Results may differ from a plain program's by a relative error of at most 0.0041.
Values may be sent and summed in bfloat16 or wider, within the bound.
No kernel may reach another device: no remote copies, remote signals or barrier semaphores. Data moves between devices by JAX's collectives and lax.ppermute only.
A program may use at most 128 MiB of HBM per device.

v0:
```python
import jax
import jax.numpy as jnp
from jax import lax
from jax.sharding import PartitionSpec as P

stat_decay = 0.95
moment_decay = 0.9
square_decay = 0.95
adam_epsilon = 1e-08
norm_epsilon = 1e-06


def per_device(partials, stats_left, stats_right, root_left, root_right, moment, second):
    owned_count = stats_left.shape[0]
    fsdp_count = lax.axis_size("fsdp")
    replica_count = lax.axis_size("dp")
    pieces = partials[0]
    block_total, row_share, block_width = pieces.shape
    spread = pieces.reshape(replica_count, block_total // replica_count, 1, row_share, block_width)
    gathered = lax.all_to_all(spread, "dp", split_axis=0, concat_axis=2, tiled=True)
    summed = jnp.sum(gathered[0].astype(jnp.float32), axis=1)
    grouped = summed.reshape(fsdp_count, owned_count, row_share, block_width)
    arrived = lax.all_to_all(grouped, "fsdp", split_axis=0, concat_axis=2, tiled=True)
    gradient = arrived.reshape(owned_count, fsdp_count * row_share, block_width)
    highest = lax.Precision.HIGHEST
    gram_left = jnp.einsum(
        "bij,bkj->bik", gradient, gradient, precision=highest, preferred_element_type=jnp.float32
    )
    gram_right = jnp.einsum(
        "bji,bjk->bik", gradient, gradient, precision=highest, preferred_element_type=jnp.float32
    )
    left_new = stat_decay * stats_left + (1.0 - stat_decay) * gram_left
    right_new = stat_decay * stats_right + (1.0 - stat_decay) * gram_right
    moment_new = moment_decay * moment + (1.0 - moment_decay) * gradient
    second_new = square_decay * second + (1.0 - square_decay) * gradient * gradient
    adam_dir = moment_new / (jnp.sqrt(second_new) + adam_epsilon)
    grad_half = gradient.astype(jnp.bfloat16)
    left_applied = jnp.einsum(
        "bij,bjk->bik", root_left, grad_half, preferred_element_type=jnp.float32
    ).astype(jnp.bfloat16)
    conditioned = jnp.einsum(
        "bij,bjk->bik", left_applied, root_right, preferred_element_type=jnp.float32
    )
    adam_norm = jnp.sqrt(jnp.sum(adam_dir * adam_dir, axis=(1, 2)))
    cond_norm = jnp.sqrt(jnp.sum(conditioned * conditioned, axis=(1, 2)))
    graft = adam_norm / (cond_norm + norm_epsilon)
    step_dir = conditioned * graft[:, None, None]
    outgoing = step_dir.reshape(owned_count, fsdp_count, row_share, block_width)
    returned = lax.all_to_all(outgoing, "fsdp", split_axis=1, concat_axis=0, tiled=True)
    step_out = returned.reshape(fsdp_count * owned_count, row_share, block_width)
    return (left_new, right_new, moment_new, second_new, step_out)


def solution(mesh):
    return jax.shard_map(
        per_device,
        mesh=mesh,
        in_specs=(
            P("dp", None, "fsdp", None),
            P(("dp", "fsdp"), None, None),
            P(("dp", "fsdp"), None, None),
            P(("dp", "fsdp"), None, None),
            P(("dp", "fsdp"), None, None),
            P(("dp", "fsdp"), None, None),
            P(("dp", "fsdp"), None, None),
        ),
        out_specs=(
            P(("dp", "fsdp"), None, None),
            P(("dp", "fsdp"), None, None),
            P(("dp", "fsdp"), None, None),
            P(("dp", "fsdp"), None, None),
            P("dp", "fsdp", None),
        ),
        check_vma=False,
    )
```

profile of v0, /device:TPU:0, one launch (start us, length us, event | category | flops | bytes accessed | tf_op | source)
XLA Modules:
  0.0 144.7 jit_solution(14028058397644902892)
XLA Ops:
  0.6 0.0 copy-start
  0.6 52.1 %all_to_all.39 = bf16[4,64,1,16,512]{4,3,1,2,0:T(8,128)(2,1)S(1)} all-to-all(bf16[4,64,1,16,512]{4,3,1,2,0:T(8,128)(2,1)} %bitcast.25), channel_id=1, replica_groups=mesh['dp'=4,'fsdp'=32] {'dp'}, dimensions={0} | all-to-all | bytes 8388608 | tf_op jit(solution)/shard_map/all_to_all | solution.py:20
  52.7 0.9 convert_reduce_fusion
  53.6 40.9 %all_to_all.40 = f32[32,2,16,512]{3,2,1,0:T(8,128)S(1)} all-to-all(f32[32,2,16,512]{3,2,1,0:T(8,128)S(1)} %bitcast.22), channel_id=1, replica_groups=mesh['dp'=4,'fsdp'=32] {'fsdp'}, dimensions={0} | all-to-all | bytes 4194304 | tf_op jit(solution)/shard_map/all_to_all | solution.py:23
  94.5 0.0 copy-start.1
  94.5 0.0 copy-start.2
  94.5 0.2 copy.17
  94.7 1.4 copy-done.1
  96.1 0.6 copy-done.2
  96.8 3.3 %multiply_reduce_fusion.1 = (f32[2]{0:T(128)S(1)}, f32[2,512,512]{2,1,0:T(8,128)}, f32[2,512,512]{2,1,0:T(8,128)}) fusion(f32[2,512,512]{2,1,0:T(8,128)S(1)} %bitcast.18, f32[2,512,512]{2,1,0:T(8,128)S(1)} %copy-done.1, f32[2,512,512]{2,1,0:T(8,128)S(1)} %copy-done.2), kind=kLoop, calls=%fused_computation.4 | loop fusion | flops 5767166 | bytes 10485768 | tf_op jit(solution)/shard_map/reduce_sum | solution.py:44
  100.0 0.0 copy-done
  100.0 4.0 %multiply_reduce_fusion = (f32[2]{0:T(128)S(1)}, f32[2,512,512]{2,1,0:T(8,128)}) fusion(bf16[2,512,512]{2,1,0:T(8,128)(2,1)S(1)} %copy-done, bf16[2,512,512]{2,1,0:T(8,128)(2,1)} %param.10, f32[2,512,512]{2,1,0:T(8,128)S(1)} %bitcast.19), kind=kOutput, calls=%fused_computation.3 | convolution fusion | flops 1075838976 | bytes 6291464 | tf_op jit(solution)/shard_map/bij,bjk->bik/dot_general | solution.py:41
  104.1 1.9 %broadcast_multiply_fusion = f32[2,512,512]{2,1,0:T(8,128)S(1)} fusion(f32[2,512,512]{2,1,0:T(8,128)} %get-tuple-element.9, f32[2]{0:T(128)S(1)} %add_divide_fusion), kind=kLoop, calls=%fused_computation.10 | loop fusion | flops 524288 | bytes 4194312 | tf_op jit(solution)/shard_map/mul | solution.py:47
  106.0 1.6 %copy.21 = f32[2,32,16,512]{3,2,0,1:T(8,128)} copy(f32[2,32,16,512]{3,2,1,0:T(8,128)S(1)} %bitcast.23) | data formatting | bytes 4194304 | tf_op jit(solution)/shard_map/reshape | solution.py:48
  107.5 4.8 %all-to-all-start.2 = ((f32[2,32,16,512]{3,2,0,1:T(8,128)}), f32[2,32,16,512]{3,2,0,1:T(8,128)}, u32[]{:S(2)}, u32[]{:S(2)}) async-start(f32[2,32,16,512]{3,2,0,1:T(8,128)} %copy.21), calls=%async_computation.2 | async-start | bytes 4194304 | tf_op jit(solution)/shard_map/all_to_all | solution.py:49
  112.3 0.0 copy-start.3
  112.3 6.1 %multiply_add_fusion.1 = f32[2,512,512]{2,1,0:T(8,128)} fusion(f32[2,512,512]{2,1,0:T(8,128)} %param.9, f32[2,512,512]{2,1,0:T(8,128)S(1)} %bitcast.20), kind=kOutput, calls=%fused_computation.6 | convolution fusion | flops 3222798336 | bytes 6291456 | tf_op jit(solution)/shard_map/bji,bjk->bik/dot_general | solution.py:29
  118.5 0.0 copy-done.3
  118.5 5.0 %multiply_add_fusion.2 = f32[2,512,512]{2,1,0:T(8,128)} fusion(f32[2,512,512]{2,1,0:T(8,128)S(1)} %copy-done.3, f32[2,512,512]{2,1,0:T(8,128)S(1)} %bitcast.21), kind=kOutput, calls=%fused_computation.7 | convolution fusion | flops 3222798336 | bytes 6291456 | tf_op jit(solution)/shard_map/bij,bkj->bik/dot_general | solution.py:26
  123.5 18.0 %all-to-all-done.2 = f32[2,32,16,512]{3,2,0,1:T(8,128)} async-done(((f32[2,32,16,512]{3,2,0,1:T(8,128)}), f32[2,32,16,512]{3,2,0,1:T(8,128)}, u32[]{:S(2)}, u32[]{:S(2)}) %all-to-all-start.2) | async-done | bytes 2097184 | tf_op jit(solution)/shard_map/all_to_all | solution.py:49
  141.4 3.2 %copy.26 = f32[64,16,512]{2,1,0:T(8,128)} copy(f32[64,16,512]{2,1,0:T(8,128)} %bitcast.8) | data formatting | bytes 4194304
  (1 shorter events, 0.0 us)
Async XLA Ops:
  0.6 99.4 %copy-start = (bf16[2,512,512]{2,1,0:T(8,128)(2,1)S(1)}, bf16[2,512,512]{2,1,0:T(8,128)(2,1)}, u32[]{:S(2)}) copy-start(bf16[2,512,512]{2,1,0:T(8,128)(2,1)} %param.11) | copy-start | bytes 3145732
  94.5 1.6 %copy-start.1 = (f32[2,512,512]{2,1,0:T(8,128)S(1)}, f32[2,512,512]{2,1,0:T(8,128)}, u32[]{:S(2)}) copy-start(f32[2,512,512]{2,1,0:T(8,128)} %param.13) | copy-start | bytes 6291460
  94.5 2.2 %copy-start.2 = (f32[2,512,512]{2,1,0:T(8,128)S(1)}, f32[2,512,512]{2,1,0:T(8,128)}, u32[]{:S(2)}) copy-start(f32[2,512,512]{2,1,0:T(8,128)} %param.12) | copy-start | bytes 6291460
  107.5 33.9 %all-to-all-start.2 = ((f32[2,32,16,512]{3,2,0,1:T(8,128)}), f32[2,32,16,512]{3,2,0,1:T(8,128)}, u32[]{:S(2)}, u32[]{:S(2)}) async-start(f32[2,32,16,512]{3,2,0,1:T(8,128)} %copy.21), calls=%async_computation.2 | async-start | bytes 4194304 | tf_op jit(solution)/shard_map/all_to_all | solution.py:49
  112.3 6.2 %copy-start.3 = (f32[2,512,512]{2,1,0:T(8,128)S(1)}, f32[2,512,512]{2,1,0:T(8,128)}, u32[]{:S(2)}) copy-start(f32[2,512,512]{2,1,0:T(8,128)} %param.8) | copy-start | bytes 6291460
where the time goes:
time: 145 us
  blocking collectives  93 us (64%)
  waiting for transfers between devices  18 us (12%)
  matrix products  15.1 us (10%)
  local copies, waits for them, and re-layouts  7.03 us (5%)
  other arithmetic  6.12 us (4%)
  starting transfers between devices  4.77 us (3%)
    all_to_all x1, blocking collectives, per_device(): lax.all_to_all(spread, 'dp', split_axis=0, concat_axis=2, tiled=True)  52.1 us
    all_to_all x1, blocking collectives, per_device(): lax.all_to_all(grouped, 'fsdp', split_axis=0, concat_axis=2, tiled=True)  40.9 us
    all_to_all x1, waiting for transfers between devices, per_device(): lax.all_to_all(outgoing, 'fsdp', split_axis=1, concat_axis=0, tiled=True)  18 us
    dot_general x1, matrix products, per_device(): jnp.einsum('bji,bjk->bik', gradient, gradient, precision=highest, preferr...  6.14 us
    unnamed x9, local copies, waits for them, and re-layouts  5.27 us
    dot_general x1, matrix products, per_device(): jnp.einsum('bij,bkj->bik', gradient, gradient, precision=highest, preferr...  4.99 us
    all_to_all x1, starting transfers between devices, per_device(): lax.all_to_all(outgoing, 'fsdp', split_axis=1, concat_axis=0, tiled=True)  4.77 us
    dot_general x1, matrix products, per_device(): jnp.einsum('bij,bjk->bik', left_applied, root_right, preferred_element_ty...  4 us
  transfers between devices with their start and end apart: 1, of which 1 were waited for; matrix products, arithmetic and copies ran while one was open for 8% of the time, Pallas kernels for 0%

commit v1 on v0

v1 whole, which is shorter than its diff:
```python
import functools

import jax
import jax.numpy as jnp
from jax import lax
from jax.experimental import pallas as pl
from jax.experimental.pallas import tpu as pltpu
from jax.sharding import Mesh, PartitionSpec as P

stat_decay = 0.95
moment_decay = 0.9
square_decay = 0.95
adam_epsilon = 1e-08
norm_epsilon = 1e-06


def split_half(values):
    high = values.astype(jnp.bfloat16)
    low = (values - high.astype(jnp.float32)).astype(jnp.bfloat16)
    return high, low


def dot(a, b):
    return jnp.dot(a, b, preferred_element_type=jnp.float32)


def pick_kernel(halves, outgoing, sem):
    core = lax.axis_index("core")
    copies = [
        pltpu.make_async_copy(halves.at[n, 1 - core], outgoing.at[n], sem.at[n])
        for n in range(halves.shape[0])
    ]
    for copy in copies:
        copy.start()
    for copy in copies:
        copy.wait()


def pick(halves):
    near, _, *rest = halves.shape
    return pl.pallas_call(
        pick_kernel,
        out_shape=jax.ShapeDtypeStruct((near, *rest), halves.dtype),
        in_specs=[pl.BlockSpec(memory_space=pl.ANY)],
        out_specs=pl.BlockSpec(memory_space=pl.ANY),
        scratch_shapes=[pltpu.SemaphoreType.DMA((near,))],
        compiler_params=pltpu.CompilerParams(vmem_limit_bytes=4 * 2**20),
        name="pick",
    )(pltpu.with_memory_space_constraint(halves, pltpu.HBM))


def preload_kernel(halves, *refs):
    count = (len(refs) - 1) // 2
    sources, targets, sem = refs[:count], refs[count : 2 * count + 1], refs[-1]
    core = lax.axis_index("core")
    near = halves.shape[0]
    copies = [
        pltpu.make_async_copy(halves.at[n, core], targets[0].at[n], sem.at[n]) for n in range(near)
    ]
    for n, (source, target) in enumerate(zip(sources, targets[1:])):
        copies.append(pltpu.make_async_copy(source, target, sem.at[near + n]))
    for copy in copies:
        copy.start()
    for copy in copies:
        copy.wait()


def preload(halves, *arrays):
    near, _, *rest = halves.shape
    size = sum(a.size * a.dtype.itemsize for a in (halves, *arrays))
    return pl.pallas_call(
        preload_kernel,
        out_shape=[pltpu.VMEM((near, *rest), halves.dtype)]
        + [pltpu.VMEM(a.shape, a.dtype) for a in arrays],
        in_specs=[pl.BlockSpec(memory_space=pl.ANY)] * (1 + len(arrays)),
        out_specs=[pl.BlockSpec(memory_space=pl.ANY)] * (1 + len(arrays)),
        scratch_shapes=[pltpu.SemaphoreType.DMA((near + len(arrays),))],
        compiler_params=pltpu.CompilerParams(vmem_limit_bytes=4 * 2**20),
        cost_estimate=pl.CostEstimate(flops=0, bytes_accessed=size, transcendentals=0),
        name="preload",
    )(*(pltpu.with_memory_space_constraint(a, pltpu.HBM) for a in (halves, *arrays)))


def pair_add_kernel(kept, swapped, total):
    rows = 8
    for n in range(kept.shape[0]):
        @pl.loop(0, kept.shape[1], step=rows)
        def _(i):
            at = (n, pl.ds(i, rows))
            total[at] = (kept[at].astype(jnp.float32) + swapped[at].astype(jnp.float32)).astype(total.dtype)


def pair_add(kept, swapped):
    return pl.pallas_call(
        pair_add_kernel,
        out_shape=pltpu.VMEM(kept.shape, kept.dtype),
        in_specs=[pl.BlockSpec(memory_space=pltpu.VMEM)] * 2,
        out_specs=pl.BlockSpec(memory_space=pltpu.VMEM),
        compiler_params=pltpu.CompilerParams(vmem_limit_bytes=8 * 2**20),
        name="pair_add",
    )(kept, pltpu.with_memory_space_constraint(swapped, pltpu.VMEM))


def direction_kernel(arrived, root_left, root_right, moment, second, step, held, sem):
    owned, size = root_left.shape[:2]
    copies = []
    for j in range(owned):
        first = arrived[0, :, j].reshape(size, size).astype(jnp.float32)
        other = arrived[1, :, j].reshape(size, size).astype(jnp.float32)
        gradient = first + other
        moment_new = moment_decay * moment[j] + (1.0 - moment_decay) * gradient
        second_new = square_decay * second[j] + (1.0 - square_decay) * gradient * gradient
        adam_dir = moment_new / (jnp.sqrt(second_new) + adam_epsilon)
        adam_sum = jnp.sum(adam_dir * adam_dir)
        high, low = split_half(gradient)
        left = root_left[j]
        right = root_right[j]
        left_high, left_low = split_half(dot(left, high) + dot(left, low))
        conditioned = dot(left_high, right) + dot(left_low, right)
        cond_sum = jnp.sum(conditioned * conditioned)
        graft = jnp.sqrt(adam_sum) / (jnp.sqrt(cond_sum) + norm_epsilon)
        held[j] = (conditioned * graft).astype(jnp.bfloat16).reshape(held.shape[1:])
        copy = pltpu.make_async_copy(held.at[j], step.at[:, j], sem.at[j])
        copy.start()
        copies.append(copy)
    for copy in copies:
        copy.wait()


def direction(arrived, root_left, root_right, moment, second):
    near, ranks, owned, share, width = arrived.shape
    held = pltpu.VMEM((owned, ranks, share, width), jnp.bfloat16)
    return pl.pallas_call(
        direction_kernel,
        out_shape=pltpu.HBM((ranks, owned, share, width), jnp.bfloat16),
        in_specs=[pl.BlockSpec(memory_space=pltpu.VMEM)] * 5,
        out_specs=pl.BlockSpec(memory_space=pl.ANY),
        scratch_shapes=[held, pltpu.SemaphoreType.DMA((owned,))],
        compiler_params=pltpu.CompilerParams(vmem_limit_bytes=24 * 2**20),
        cost_estimate=pl.CostEstimate(
            flops=owned * 8 * width**3, bytes_accessed=11 * 2**20, transcendentals=0
        ),
        name="direction",
    )(arrived, root_left, root_right, moment, second)


def gram(high, low, contract):
    def product(a, b):
        return lax.dot_general(
            a, b, (((contract,), (contract,)), ((), ())), preferred_element_type=jnp.float32
        )

    return product(high, high) + product(high, low) + product(low, high)


def statistics_kernel(
    arrived, stats_left, stats_right, moment, second, left_new, right_new, moment_new, second_new
):
    size = stats_left.shape[-1]
    first = arrived[0, :, 0].reshape(size, size).astype(jnp.float32)
    other = arrived[1, :, 0].reshape(size, size).astype(jnp.float32)
    gradient = first + other
    moment_new[0] = moment_decay * moment[0] + (1.0 - moment_decay) * gradient
    second_new[0] = square_decay * second[0] + (1.0 - square_decay) * gradient * gradient
    high, low = split_half(gradient)
    left_new[0] = stat_decay * stats_left[0] + (1.0 - stat_decay) * gram(high, low, 1)
    right_new[0] = stat_decay * stats_right[0] + (1.0 - stat_decay) * gram(high, low, 0)


def statistics(arrived, stats_left, stats_right, moment, second):
    near, ranks, owned, share, width = arrived.shape
    square = pl.BlockSpec((1, width, width), lambda j: (j, 0, 0))
    fixed = [pltpu.with_memory_space_constraint(a, pltpu.HBM) for a in (stats_left, stats_right, moment, second)]
    return pl.pallas_call(
        statistics_kernel,
        grid=(owned,),
        out_shape=[jax.ShapeDtypeStruct(stats_left.shape, jnp.float32)] * 4,
        in_specs=[pl.BlockSpec((near, ranks, 1, share, width), lambda j: (0, 0, j, 0, 0))] + [square] * 4,
        out_specs=[square] * 4,
        compiler_params=pltpu.CompilerParams(vmem_limit_bytes=40 * 2**20),
        cost_estimate=pl.CostEstimate(
            flops=owned * 12 * width**3, bytes_accessed=18 * 2**20, transcendentals=0
        ),
        name="statistics",
    )(arrived, *fixed)


def widen_kernel(narrow, wide):
    wide[...] = narrow[...].astype(jnp.float32)


def widen(narrow):
    rows = 16
    count, share, width = narrow.shape
    spec = pl.BlockSpec((rows, share, width), lambda i: (i, 0, 0))
    return pl.pallas_call(
        widen_kernel,
        grid=(count // rows,),
        out_shape=jax.ShapeDtypeStruct(narrow.shape, jnp.float32),
        in_specs=[spec],
        out_specs=spec,
        compiler_params=pltpu.CompilerParams(vmem_limit_bytes=16 * 2**20),
        name="widen",
    )(narrow)


def per_device(partials, stats_left, stats_right, root_left, root_right, moment, second):
    owned_count = stats_left.shape[0]
    fsdp_count = lax.axis_size("fsdp")
    near_count = lax.axis_size("near")
    pieces = partials[0]
    _, row_share, block_width = pieces.shape
    halves = pieces.reshape(near_count, 2, fsdp_count * owned_count, row_share, block_width)
    swapped = lax.ppermute(pick(halves), "core", [(0, 1), (1, 0)])
    kept, left_here, right_here, moment_here, second_here = preload(
        halves, root_left, root_right, moment, second
    )
    pair_sum = pair_add(kept, swapped)
    grouped = pair_sum.reshape(near_count * fsdp_count, owned_count, row_share, block_width)
    arrived = lax.all_to_all(grouped, ("near", "fsdp"), split_axis=0, concat_axis=0, tiled=True)
    arrived = arrived.reshape(near_count, fsdp_count, owned_count, row_share, block_width)
    step = direction(arrived, left_here, right_here, moment_here, second_here)
    returned = lax.all_to_all(step, "fsdp", split_axis=0, concat_axis=0, tiled=True)
    step_out = widen(returned.reshape(fsdp_count * owned_count, row_share, block_width))
    news = statistics(arrived, stats_left, stats_right, moment, second)
    return (*news, step_out)


def solution(mesh):
    fine = Mesh(mesh.devices.reshape(2, 2, -1), ("near", "core", "fsdp"))
    owned = P(("near", "core", "fsdp"), None, None)
    return jax.shard_map(
        per_device,
        mesh=fine,
        in_specs=(P(("near", "core"), None, "fsdp", None), owned, owned, owned, owned, owned, owned),
        out_specs=(owned, owned, owned, owned, P(("near", "core"), "fsdp", None)),
        check_vma=False,
    )
```

time: 145 us -> 78.5 us (0.54)
  blocking collectives: 93 us -> 40.9 us
  Pallas kernels: 0 us -> 20.4 us
  matrix products: 15.1 us -> 0 us
  local copies, waits for them, and re-layouts: 7.03 us -> 0 us
  waiting for transfers between devices: 18 us -> 11.8 us
  other arithmetic: 6.12 us -> 0 us
    all_to_all x2 -> x1, blocking collectives: 93 us -> 40.9 us  [per_device(): lax.all_to_all(grouped, ('near', 'fsdp'), split_axis=0, concat_axis=0, ti...]
    pallas_call x0 -> x6, Pallas kernels: none -> 20.4 us  [the longest x1 7.86 us: statistics(): pl.pallas_call(statistics_kernel, grid=(owned,), out_shape=[jax.ShapeDtyp...]
    dot_general x3 -> x0, matrix products: 15.1 us -> none  [the longest x1 6.14 us: per_device(): jnp.einsum('bji,bjk->bik', gradient, gradient, precision=highest, preferr...]
    all_to_all x1, waiting for transfers between devices: 18 us -> 11.2 us  [per_device(): lax.all_to_all(step, 'fsdp', split_axis=0, concat_axis=0, tiled=True)]
    unnamed x9 -> x0, local copies, waits for them, and re-layouts: 5.27 us -> none
    reduce_sum x2 -> x0, other arithmetic: 4.21 us -> none  [the longest x1 3.29 us: per_device(): adam_norm = jnp.sqrt(jnp.sum(adam_dir * adam_dir, axis=(1, 2)))]
    mul x1 -> x0, other arithmetic: 1.89 us -> none  [per_device(): step_dir = conditioned * graft[:, None, None]]
    reshape x1 -> x0, local copies, waits for them, and re-layouts: 1.58 us -> none  [per_device(): outgoing = step_dir.reshape(owned_count, fsdp_count, row_share, block_width)]
  transfers between devices with their start and end apart: 1 -> 2, of which waited for: 1 -> 2; matrix products, arithmetic and copies ran while one was open for 8% -> 0% of each run, Pallas kernels for 0% -> 15%
where the time goes in v1:
time: 78.5 us; the launch traced here: 78.2 us
  blocking collectives  40.9 us (52%)
  Pallas kernels  20.4 us (26%)
  waiting for transfers between devices  11.8 us (15%)
  starting transfers between devices  4.46 us (6%)
    all_to_all x1, blocking collectives, per_device(): lax.all_to_all(grouped, ('near', 'fsdp'), split_axis=0, concat_axis=0, ti...  40.9 us
    all_to_all x1, waiting for transfers between devices, per_device(): lax.all_to_all(step, 'fsdp', split_axis=0, concat_axis=0, tiled=True)  11.2 us
    pallas_call x1, Pallas kernels, statistics(): pl.pallas_call(statistics_kernel, grid=(owned,), out_shape=[jax.ShapeDtyp...  7.86 us
    pallas_call x1, Pallas kernels, direction(): pl.pallas_call(direction_kernel, out_shape=pltpu.HBM((ranks, owned, share...  5.09 us
    all_to_all x1, starting transfers between devices, per_device(): lax.all_to_all(step, 'fsdp', split_axis=0, concat_axis=0, tiled=True)  4.37 us
    pallas_call x1, Pallas kernels, preload(): pl.pallas_call(preload_kernel, out_shape=[pltpu.VMEM((near, *rest), halve...  3.55 us
    pallas_call x1, Pallas kernels, widen(): pl.pallas_call(widen_kernel, grid=(count // rows,), out_shape=jax.ShapeDt...  1.83 us
  transfers between devices with their start and end apart: 2, of which 2 were waited for; matrix products, arithmetic and copies ran while one was open for 0% of the time, Pallas kernels for 15%

profile of v1, /device:TPU:0, one launch (start us, length us, event | category | flops | bytes accessed | tf_op | source)
XLA Modules:
  0.0 78.2 jit_solution(657949684918208205)
XLA Ops:
  0.6 1.6 %pick.1 = bf16[2,64,16,512]{3,2,1,0:T(8,128)(2,1)S(1)} custom-call(bf16[2,2,64,16,512]{4,3,2,1,0:T(8,128)(2,1)} %bitcast.8), custom_call_target="tpu_custom_call" | custom-call | tf_op jit(solution)/shard_map/pick/pallas_call | solution.py:41
  2.2 0.1 collective-permute-start
  2.3 3.5 %preload.1 = (bf16[2,64,16,512]{3,2,1,0:T(8,128)(2,1)S(1)}, bf16[2,512,512]{2,1,0:T(8,128)(2,1)S(1)}, bf16[2,512,512]{2,1,0:T(8,128)(2,1)S(1)}, f32[2,512,512]{2,1,0:T(8,128)S(1)}, f32[2,512,512]{2,1,0:T(8,128)S(1)}) custom-call(bf16[2,2,64,16,512]{4,3,2,1,0:T(8,128)(2,1)} %bitcast.9, bf16[2,512,512]{2,1,0:T(8,128)(2,1)} %refs_0_.1, ...), custom_call_target="tpu_custom_call" | custom-call | bytes 10485760 | tf_op jit(solution)/shard_map/preload/pallas_call | solution.py:71
  5.9 0.6 collective-permute-done.swapped
  6.4 0.5 pair_add.1
  7.0 40.9 %all_to_all.10 = bf16[64,2,16,512]{3,2,1,0:T(8,128)(2,1)S(1)} all-to-all(bf16[64,2,16,512]{3,2,1,0:T(8,128)(2,1)S(1)} %bitcast.4), channel_id=1, replica_groups=mesh['near'=2,'core'=2,'fsdp'=32] {'near','fsdp'}, dimensions={0} | all-to-all | bytes 4194304 | tf_op jit(solution)/shard_map/all_to_all | solution.py:220
  47.9 5.1 %direction.1 = bf16[32,2,16,512]{3,2,1,0:T(8,128)(2,1)} custom-call(bf16[2,32,2,16,512]{4,3,2,1,0:T(8,128)(2,1)S(1)} %bitcast.5, bf16[2,512,512]{2,1,0:T(8,128)(2,1)S(1)} %get-tuple-element.19.root_left, bf16[2,512,512]{2,1,0:T(8,128)(2,1)S(1)} %get-tuple-element.20.root_right, f32[2,512,512]{2,1,0:T(8,128)S(1)} %get-tuple-element.21.moment, ...), custom_call_target="tpu_custom_call" | custom-call | flops 2147483648 | bytes 11534336 | tf_op jit(solution)/shard_map/direction/pallas_call | solution.py:133
  53.0 4.4 %all-to-all-start.1 = ((bf16[32,2,16,512]{3,2,1,0:T(8,128)(2,1)}), bf16[32,2,16,512]{3,2,1,0:T(8,128)(2,1)S(1)}, u32[]{:S(2)}, u32[]{:S(2)}) async-start(bf16[32,2,16,512]{3,2,1,0:T(8,128)(2,1)} %direction.1), calls=%async_computation.1 | async-start | bytes 2097152 | tf_op jit(solution)/shard_map/all_to_all | solution.py:223
  57.4 7.9 %statistics.1 = (f32[2,512,512]{2,1,0:T(8,128)}, f32[2,512,512]{2,1,0:T(8,128)}, f32[2,512,512]{2,1,0:T(8,128)}, f32[2,512,512]{2,1,0:T(8,128)}) custom-call(bf16[2,32,2,16,512]{4,3,2,1,0:T(8,128)(2,1)S(1)} %bitcast.6, f32[2,512,512]{2,1,0:T(8,128)} %stats_left.1, f32[2,512,512]{2,1,0:T(8,128)} %stats_right.1, f32[2,512,512]{2,1,0:T(8,128)} %moment.1, ...), custom_call_target="tpu_custom_call" | custom-call | flops 3221225472 | bytes 18874368 | tf_op jit(solution)/shard_map/statistics/pallas_call | solution.py:174
  65.2 11.2 %all-to-all-done.1 = bf16[32,2,16,512]{3,2,1,0:T(8,128)(2,1)S(1)} async-done(((bf16[32,2,16,512]{3,2,1,0:T(8,128)(2,1)}), bf16[32,2,16,512]{3,2,1,0:T(8,128)(2,1)S(1)}, u32[]{:S(2)}, u32[]{:S(2)}) %all-to-all-start.1) | async-done | bytes 1048608 | tf_op jit(solution)/shard_map/all_to_all | solution.py:223
  76.4 1.8 %widen.1 = f32[64,16,512]{2,1,0:T(8,128)} custom-call(bf16[64,16,512]{2,1,0:T(8,128)(2,1)S(1)} %bitcast.7), custom_call_target="tpu_custom_call" | custom-call | tf_op jit(solution)/shard_map/widen/pallas_call | solution.py:196
Async XLA Ops:
  2.2 4.2 %collective-permute-start = (bf16[2,64,16,512]{3,2,1,0:T(8,128)(2,1)S(1)}, bf16[2,64,16,512]{3,2,1,0:T(8,128)(2,1)S(1)}, u32[]{:S(2)}, u32[]{:S(2)}) collective-permute-start(bf16[2,64,16,512]{3,2,1,0:T(8,128)(2,1)S(1)} %pick.1), channel_id=1, source_target_pairs={{0,32},{32,0},{1,33},{33,1},{2,34},{34,2},{3,35},{35,3},{4,36},{36... | collective-permute-start | bytes 6291464 | tf_op jit(solution)/shard_map/ppermute | solution.py:214
  53.0 23.4 %all-to-all-start.1 = ((bf16[32,2,16,512]{3,2,1,0:T(8,128)(2,1)}), bf16[32,2,16,512]{3,2,1,0:T(8,128)(2,1)S(1)}, u32[]{:S(2)}, u32[]{:S(2)}) async-start(bf16[32,2,16,512]{3,2,1,0:T(8,128)(2,1)} %direction.1), calls=%async_computation.1 | async-start | bytes 2097152 | tf_op jit(solution)/shard_map/all_to_all | solution.py:223

commit v2 on v1

v2 whole, which is shorter than its diff:
```python
import functools

import jax
import jax.numpy as jnp
from jax import lax
from jax.experimental import pallas as pl
from jax.experimental.pallas import tpu as pltpu
from jax.sharding import Mesh, PartitionSpec as P

stat_decay = 0.95
moment_decay = 0.9
square_decay = 0.95
adam_epsilon = 1e-08
norm_epsilon = 1e-06
every_axis = ("near", "core", "fsdp")


def split_half(values):
    high = values.astype(jnp.bfloat16)
    low = (values - high.astype(jnp.float32)).astype(jnp.bfloat16)
    return high, low


def dot(a, b):
    return jnp.dot(a, b, preferred_element_type=jnp.float32)


def pick_kernel(halves, outgoing, sem):
    core = lax.axis_index("core")
    near, cuts = sem.shape
    count = halves.shape[2] // cuts
    copies = []
    for n in range(near):
        for c in range(cuts):
            at = pl.ds(c * count, count)
            copies.append(
                pltpu.make_async_copy(halves.at[n, 1 - core, at], outgoing.at[n, at], sem.at[n, c])
            )
    for copy in copies:
        copy.start()
    for copy in copies:
        copy.wait()


def pick(halves):
    near, _, *rest = halves.shape
    return pl.pallas_call(
        pick_kernel,
        out_shape=jax.ShapeDtypeStruct((near, *rest), halves.dtype),
        in_specs=[pl.BlockSpec(memory_space=pl.ANY)],
        out_specs=pl.BlockSpec(memory_space=pl.ANY),
        scratch_shapes=[pltpu.SemaphoreType.DMA((near, 4))],
        compiler_params=pltpu.CompilerParams(vmem_limit_bytes=4 * 2**20),
        name="pick",
    )(pltpu.with_memory_space_constraint(halves, pltpu.HBM))


def preload_kernel(halves, *refs):
    count = (len(refs) - 1) // 2
    sources, targets, sem = refs[:count], refs[count : 2 * count + 1], refs[-1]
    core = lax.axis_index("core")
    near = halves.shape[0]
    copies = [
        pltpu.make_async_copy(halves.at[n, core], targets[0].at[n], sem.at[n]) for n in range(near)
    ]
    for n, (source, target) in enumerate(zip(sources, targets[1:])):
        copies.append(pltpu.make_async_copy(source, target, sem.at[near + n]))
    for copy in copies:
        copy.start()
    for copy in copies:
        copy.wait()


def preload(halves, *arrays):
    near, _, *rest = halves.shape
    size = sum(a.size * a.dtype.itemsize for a in (halves, *arrays))
    return pl.pallas_call(
        preload_kernel,
        out_shape=[pltpu.VMEM((near, *rest), halves.dtype)]
        + [pltpu.VMEM(a.shape, a.dtype) for a in arrays],
        in_specs=[pl.BlockSpec(memory_space=pl.ANY)] * (1 + len(arrays)),
        out_specs=[pl.BlockSpec(memory_space=pl.ANY)] * (1 + len(arrays)),
        scratch_shapes=[pltpu.SemaphoreType.DMA((near + len(arrays),))],
        compiler_params=pltpu.CompilerParams(vmem_limit_bytes=4 * 2**20),
        cost_estimate=pl.CostEstimate(flops=0, bytes_accessed=size, transcendentals=0),
        name="preload",
    )(*(pltpu.with_memory_space_constraint(a, pltpu.HBM) for a in (halves, *arrays)))


def pair_add_kernel(kept, swapped, total, *, turn):
    rows = 8
    count = total.shape[0]

    def add(source, size, target):
        at = pl.ds(source, size)
        both = kept[at].astype(jnp.float32) + swapped[at].astype(jnp.float32)
        total[pl.ds(target, size)] = both.astype(total.dtype)

    @pl.loop(0, count - rows, step=rows)
    def _(i):
        add(i, rows, i + turn)

    add(count - rows, rows - turn, count - rows + turn)
    add(count - turn, turn, 0)


def pair_add(kept, swapped, turn):
    return pl.pallas_call(
        functools.partial(pair_add_kernel, turn=turn),
        out_shape=pltpu.VMEM(kept.shape, kept.dtype),
        in_specs=[pl.BlockSpec(memory_space=pltpu.VMEM)] * 2,
        out_specs=pl.BlockSpec(memory_space=pltpu.VMEM),
        compiler_params=pltpu.CompilerParams(vmem_limit_bytes=8 * 2**20),
        name="pair_add",
    )(kept, pltpu.with_memory_space_constraint(swapped, pltpu.VMEM))


def pair_sums(arrived, j):
    count, _, share, width = arrived.shape
    half = count // 2
    size = half * share
    first = arrived[1 : half + 1, j].reshape(size, width)
    most = arrived[half + 1 :, j].reshape(size - share, width)
    other = jnp.concatenate([most, arrived[0, j]], axis=0)
    return first, other


def direction_kernel(arrived, root_left, root_right, moment, second, step, held, sem):
    owned = root_left.shape[0]
    ranks = held.shape[1]
    cuts = sem.shape[1] - 1
    copies = []
    for j in range(owned):
        first, other = pair_sums(arrived, j)
        left = root_left[j]
        right = root_right[j]
        left_high, left_low = split_half(dot(left, first) + dot(left, other))
        gradient = first.astype(jnp.float32) + other.astype(jnp.float32)
        moment_new = moment_decay * moment[j] + (1.0 - moment_decay) * gradient
        second_new = square_decay * second[j] + (1.0 - square_decay) * gradient * gradient
        divisor = second_new * lax.rsqrt(second_new) + adam_epsilon
        adam_dir = moment_new * lax.rsqrt(divisor * divisor)
        adam_sum = jnp.sum(adam_dir * adam_dir)
        conditioned = dot(left_high, right) + dot(left_low, right)
        cond_sum = jnp.sum(conditioned * conditioned)
        graft = jnp.sqrt(adam_sum) / (jnp.sqrt(cond_sum) + norm_epsilon)
        held[j] = (conditioned * graft).astype(jnp.bfloat16).reshape(held.shape[1:])
        edges = [c * (ranks // cuts) for c in range(cuts)] + [ranks - 1, ranks]
        for c in range(cuts + 1):
            start, size = edges[c], edges[c + 1] - edges[c]
            target = (start + 1) % ranks
            copy = pltpu.make_async_copy(
                held.at[j, pl.ds(start, size)], step.at[pl.ds(target, size), j], sem.at[j, c]
            )
            copy.start()
            copies.append(copy)
    for copy in copies:
        copy.wait()


def direction(arrived, root_left, root_right, moment, second):
    count, owned, share, width = arrived.shape
    ranks = count // 2
    return pl.pallas_call(
        direction_kernel,
        out_shape=pltpu.HBM((ranks, owned, share, width), jnp.bfloat16),
        in_specs=[pl.BlockSpec(memory_space=pltpu.VMEM)] * 5,
        out_specs=pl.BlockSpec(memory_space=pl.ANY),
        scratch_shapes=[
            pltpu.VMEM((owned, ranks, share, width), jnp.bfloat16),
            pltpu.SemaphoreType.DMA((owned, 5)),
        ],
        compiler_params=pltpu.CompilerParams(vmem_limit_bytes=24 * 2**20),
        cost_estimate=pl.CostEstimate(
            flops=owned * 8 * width**3, bytes_accessed=11 * 2**20, transcendentals=0
        ),
        name="direction",
    )(arrived, root_left, root_right, moment, second)


def gram(high, low, contract):
    def product(a, b):
        return lax.dot_general(
            a, b, (((contract,), (contract,)), ((), ())), preferred_element_type=jnp.float32
        )

    return product(high, high) + product(high, low) + product(low, high)


def statistics_kernel(
    arrived, stats_left, stats_right, moment, second, left_new, right_new, moment_new, second_new
):
    first, other = pair_sums(arrived, 0)
    gradient = first.astype(jnp.float32) + other.astype(jnp.float32)
    moment_new[0] = moment_decay * moment[0] + (1.0 - moment_decay) * gradient
    second_new[0] = square_decay * second[0] + (1.0 - square_decay) * gradient * gradient
    high, low = split_half(gradient)
    left_new[0] = stat_decay * stats_left[0] + (1.0 - stat_decay) * gram(high, low, 1)
    right_new[0] = stat_decay * stats_right[0] + (1.0 - stat_decay) * gram(high, low, 0)


def statistics(arrived, stats_left, stats_right, moment, second):
    count, owned, share, width = arrived.shape
    square = pl.BlockSpec((1, width, width), lambda j: (j, 0, 0))
    fixed = [pltpu.with_memory_space_constraint(a, pltpu.HBM) for a in (stats_left, stats_right, moment, second)]
    return pl.pallas_call(
        statistics_kernel,
        grid=(owned,),
        out_shape=[jax.ShapeDtypeStruct(stats_left.shape, jnp.float32)] * 4,
        in_specs=[pl.BlockSpec((count, 1, share, width), lambda j: (0, j, 0, 0))] + [square] * 4,
        out_specs=[square] * 4,
        compiler_params=pltpu.CompilerParams(vmem_limit_bytes=40 * 2**20),
        cost_estimate=pl.CostEstimate(
            flops=owned * 12 * width**3, bytes_accessed=18 * 2**20, transcendentals=0
        ),
        name="statistics",
    )(arrived, *fixed)


def widen_kernel(narrow, wide, held, sem):
    ranks = narrow.shape[0]
    cuts = sem.shape[0]
    size = ranks // cuts
    copies = []
    for c in range(cuts):
        at = pl.ds(c * size, size)
        if c < cuts - 1:
            held[at] = narrow[pl.ds(c * size + 1, size)].astype(jnp.float32)
        else:
            held[pl.ds(c * size, size - 1)] = narrow[pl.ds(c * size + 1, size - 1)].astype(jnp.float32)
            held[ranks - 1] = narrow[0].astype(jnp.float32)
        copy = pltpu.make_async_copy(held.at[at], wide.at[at], sem.at[c])
        copy.start()
        copies.append(copy)
    for copy in copies:
        copy.wait()


def widen(narrow):
    return pl.pallas_call(
        widen_kernel,
        out_shape=pltpu.HBM(narrow.shape, jnp.float32),
        in_specs=[pl.BlockSpec(memory_space=pltpu.VMEM)],
        out_specs=pl.BlockSpec(memory_space=pl.ANY),
        scratch_shapes=[
            pltpu.VMEM(narrow.shape, jnp.float32),
            pltpu.SemaphoreType.DMA((4,)),
        ],
        compiler_params=pltpu.CompilerParams(vmem_limit_bytes=8 * 2**20),
        name="widen",
    )(narrow)


def last_first(ranks):
    return ranks[-1:] + ranks[:-1]


def exchange(chunks, groups):
    return lax.all_to_all(
        chunks, every_axis, split_axis=0, concat_axis=0, tiled=True, axis_index_groups=groups
    )


def per_device(partials, stats_left, stats_right, root_left, root_right, moment, second):
    owned_count = stats_left.shape[0]
    fsdp_count = lax.axis_size("fsdp")
    near_count = lax.axis_size("near")
    pieces = partials[0]
    _, row_share, block_width = pieces.shape
    block = (row_share, block_width)
    halves = pieces.reshape(near_count, 2, fsdp_count * owned_count, *block)
    swapped = lax.ppermute(pick(halves), "core", [(0, 1), (1, 0)])
    kept, left_here, right_here, moment_here, second_here = preload(
        halves, root_left, root_right, moment, second
    )
    pair_sum = pair_add(kept.reshape(-1, *block), swapped.reshape(-1, *block), owned_count)

    def rank(near, core, fsdp):
        return (near * 2 + core) * fsdp_count + fsdp

    gather_groups = [
        last_first([rank(near, core, f) for near in range(near_count) for f in range(fsdp_count)])
        for core in range(2)
    ]
    return_groups = [
        last_first([rank(near, core, f) for f in range(fsdp_count)])
        for near in range(near_count)
        for core in range(2)
    ]
    arrived = exchange(pair_sum.reshape(-1, owned_count, *block), gather_groups)
    step = direction(arrived, left_here, right_here, moment_here, second_here)
    returned = exchange(step, return_groups)
    step_out = widen(returned).reshape(-1, *block)
    news = statistics(arrived, stats_left, stats_right, moment, second)
    return (*news, step_out)


def solution(mesh):
    fine = Mesh(mesh.devices.reshape(2, 2, -1), every_axis)
    owned = P(every_axis, None, None)
    return jax.shard_map(
        per_device,
        mesh=fine,
        in_specs=(P(("near", "core"), None, "fsdp", None), owned, owned, owned, owned, owned, owned),
        out_specs=(owned, owned, owned, owned, P(("near", "core"), "fsdp", None)),
        check_vma=False,
    )
```

time: 78.5 us -> 73.1 us (0.931)
  waiting for transfers between devices: 11.8 us -> 4.53 us
  starting transfers between devices: 4.46 us -> 9.68 us
  blocking collectives: 40.9 us -> 37.8 us
  Pallas kernels: 20.4 us -> 19.5 us
    all_to_all x1, waiting for transfers between devices: 11.2 us -> 3.94 us  [exchange(): lax.all_to_all(chunks, every_axis, split_axis=0, concat_axis=0, tiled=Tru...]
    all_to_all x1, starting transfers between devices: 4.37 us -> 9.59 us  [exchange(): lax.all_to_all(chunks, every_axis, split_axis=0, concat_axis=0, tiled=Tru...]
    all_to_all x1, blocking collectives: 40.9 us -> 37.8 us  [exchange(): lax.all_to_all(chunks, every_axis, split_axis=0, concat_axis=0, tiled=Tru...]
  transfers between devices with their start and end apart: 2 -> 2, of which waited for: 2 -> 2; matrix products, arithmetic and copies ran while one was open for 0% -> 0% of each run, Pallas kernels for 15% -> 16%
where the time goes in v2:
time: 73.1 us; the launch traced here: 72.2 us
  blocking collectives  37.8 us (52%)
  Pallas kernels  19.5 us (27%)
  starting transfers between devices  9.68 us (13%)
  waiting for transfers between devices  4.53 us (6%)
    all_to_all x1, blocking collectives, exchange(): lax.all_to_all(chunks, every_axis, split_axis=0, concat_axis=0, tiled=Tru...  37.8 us
    all_to_all x1, starting transfers between devices, exchange(): lax.all_to_all(chunks, every_axis, split_axis=0, concat_axis=0, tiled=Tru...  9.59 us
    pallas_call x1, Pallas kernels, statistics(): pl.pallas_call(statistics_kernel, grid=(owned,), out_shape=[jax.ShapeDtyp...  7.87 us
    pallas_call x1, Pallas kernels, direction(): pl.pallas_call(direction_kernel, out_shape=pltpu.HBM((ranks, owned, share...  4.55 us
    all_to_all x1, waiting for transfers between devices, exchange(): lax.all_to_all(chunks, every_axis, split_axis=0, concat_axis=0, tiled=Tru...  3.94 us
    pallas_call x1, Pallas kernels, preload(): pl.pallas_call(preload_kernel, out_shape=[pltpu.VMEM((near, *rest), halve...  3.55 us
    pallas_call x1, Pallas kernels, pick(): pl.pallas_call(pick_kernel, out_shape=jax.ShapeDtypeStruct((near, *rest),...  1.58 us
  transfers between devices with their start and end apart: 2, of which 2 were waited for; matrix products, arithmetic and copies ran while one was open for 0% of the time, Pallas kernels for 16%

profile of v2, /device:TPU:0, one launch (start us, length us, event | category | flops | bytes accessed | tf_op | source)
XLA Modules:
  0.0 72.2 jit_solution(3849389723184359637)
XLA Ops:
  0.6 1.6 %pick.1 = bf16[2,64,16,512]{3,2,1,0:T(8,128)(2,1)S(1)} custom-call(bf16[2,2,64,16,512]{4,3,2,1,0:T(8,128)(2,1)} %bitcast.8), custom_call_target="tpu_custom_call" | custom-call | tf_op jit(solution)/shard_map/pick/pallas_call | solution.py:47
  2.2 0.1 collective-permute-start
  2.3 3.5 %preload.1 = (bf16[2,64,16,512]{3,2,1,0:T(8,128)(2,1)S(1)}, bf16[2,512,512]{2,1,0:T(8,128)(2,1)S(1)}, bf16[2,512,512]{2,1,0:T(8,128)(2,1)S(1)}, f32[2,512,512]{2,1,0:T(8,128)S(1)}, f32[2,512,512]{2,1,0:T(8,128)S(1)}) custom-call(bf16[2,2,64,16,512]{4,3,2,1,0:T(8,128)(2,1)} %bitcast.9, bf16[2,512,512]{2,1,0:T(8,128)(2,1)} %refs_0_.1, ...), custom_call_target="tpu_custom_call" | custom-call | bytes 10485760 | tf_op jit(solution)/shard_map/preload/pallas_call | solution.py:77
  5.9 0.6 collective-permute-done
  6.5 0.5 pair_add.1
  7.0 37.8 %all_to_all.10.arrived = bf16[64,2,16,512]{3,2,1,0:T(8,128)(2,1)S(1)} all-to-all(bf16[64,2,16,512]{3,2,1,0:T(8,128)(2,1)S(1)} %bitcast.5), channel_id=1, replica_groups={{95,0,1,2,3,4,5,6,7,8,9,10,11,12,13,14,15,16,17,18,19,20,21,22,23,24,25..., dimensions={0} | all-to-all | bytes 4194304 | tf_op jit(solution)/shard_map/all_to_all | solution.py:259
  44.8 4.6 %direction.1 = bf16[32,2,16,512]{3,2,1,0:T(8,128)(2,1)} custom-call(bf16[64,2,16,512]{3,2,1,0:T(8,128)(2,1)S(1)} %all_to_all.10.arrived, bf16[2,512,512]{2,1,0:T(8,128)(2,1)S(1)} %get-tuple-element.19.root_left, bf16[2,512,512]{2,1,0:T(8,128)(2,1)S(1)} %get-tuple-element.20.root_right, f32[2,512,512]{2,1,0:T(8,128)S(1)} %get-tuple-element.21.moment, ...), custom_call_target="tpu_custom_call" | custom-call | flops 2147483648 | bytes 11534336 | tf_op jit(solution)/shard_map/direction/pallas_call | solution.py:164
  49.4 9.6 %all-to-all-start.1 = ((bf16[32,2,16,512]{3,2,1,0:T(8,128)(2,1)}), bf16[32,2,16,512]{3,2,1,0:T(8,128)(2,1)S(1)}, u32[]{:S(2)}, u32[]{:S(2)}) async-start(bf16[32,2,16,512]{3,2,1,0:T(8,128)(2,1)} %direction.1), calls=%async_computation.1 | async-start | bytes 2097152 | tf_op jit(solution)/shard_map/all_to_all | solution.py:259
  59.0 7.9 %statistics.1 = (f32[2,512,512]{2,1,0:T(8,128)}, f32[2,512,512]{2,1,0:T(8,128)}, f32[2,512,512]{2,1,0:T(8,128)}, f32[2,512,512]{2,1,0:T(8,128)}) custom-call(bf16[64,2,16,512]{3,2,1,0:T(8,128)(2,1)S(1)} %all_to_all.10.arrived, f32[2,512,512]{2,1,0:T(8,128)} %stats_left.1, f32[2,512,512]{2,1,0:T(8,128)} %stats_right.1, f32[2,512,512]{2,1,0:T(8,128)} %moment.1, ...), custom_call_target="tpu_custom_call" | custom-call | flops 3221225472 | bytes 18874368 | tf_op jit(solution)/shard_map/statistics/pallas_call | solution.py:206
  66.8 3.9 %all-to-all-done.1.narrow = bf16[32,2,16,512]{3,2,1,0:T(8,128)(2,1)S(1)} async-done(((bf16[32,2,16,512]{3,2,1,0:T(8,128)(2,1)}), bf16[32,2,16,512]{3,2,1,0:T(8,128)(2,1)S(1)}, u32[]{:S(2)}, u32[]{:S(2)}) %all-to-all-start.1) | async-done | bytes 1048608 | tf_op jit(solution)/shard_map/all_to_all | solution.py:259
  70.8 1.4 %widen.1 = f32[32,2,16,512]{3,2,1,0:T(8,128)} custom-call(bf16[32,2,16,512]{3,2,1,0:T(8,128)(2,1)S(1)} %all-to-all-done.1.narrow), custom_call_target="tpu_custom_call" | custom-call | tf_op jit(solution)/shard_map/widen/pallas_call | solution.py:240
Async XLA Ops:
  2.2 4.2 %collective-permute-start = (bf16[2,64,16,512]{3,2,1,0:T(8,128)(2,1)S(1)}, bf16[2,64,16,512]{3,2,1,0:T(8,128)(2,1)S(1)}, u32[]{:S(2)}, u32[]{:S(2)}) collective-permute-start(bf16[2,64,16,512]{3,2,1,0:T(8,128)(2,1)S(1)} %pick.1), channel_id=1, source_target_pairs={{0,32},{32,0},{1,33},{33,1},{2,34},{34,2},{3,35},{35,3},{4,36},{36... | collective-permute-start | bytes 6291464 | tf_op jit(solution)/shard_map/ppermute | solution.py:272
  49.4 21.4 %all-to-all-start.1 = ((bf16[32,2,16,512]{3,2,1,0:T(8,128)(2,1)}), bf16[32,2,16,512]{3,2,1,0:T(8,128)(2,1)S(1)}, u32[]{:S(2)}, u32[]{:S(2)}) async-start(bf16[32,2,16,512]{3,2,1,0:T(8,128)(2,1)} %direction.1), calls=%async_computation.1 | async-start | bytes 2097152 | tf_op jit(solution)/shard_map/all_to_all | solution.py:259

commit v3 on v2

--- a/solution.py
+++ b/solution.py
@@ -129,19 +129,36 @@
     owned = root_left.shape[0]
     ranks = held.shape[1]
     cuts = sem.shape[1] - 1
+    width = root_left.shape[-1]
+    half, quarter = width // 2, width // 4
     copies = []
     for j in range(owned):
         first, other = pair_sums(arrived, j)
+
+        def adam_squares(part):
+            at = slice(part * quarter, (part + 1) * quarter)
+            gradient = first[at].astype(jnp.float32) + other[at].astype(jnp.float32)
+            moment_new = moment_decay * moment[j, at] + (1.0 - moment_decay) * gradient
+            second_new = square_decay * second[j, at] + (1.0 - square_decay) * gradient * gradient
+            divisor = second_new * lax.rsqrt(second_new) + adam_epsilon
+            adam_dir = moment_new * lax.rsqrt(divisor * divisor)
+            return jnp.sum((adam_dir * adam_dir).reshape(quarter // 8, 8, width), axis=0)
+
         left = root_left[j]
         right = root_right[j]
-        left_high, left_low = split_half(dot(left, first) + dot(left, other))
-        gradient = first.astype(jnp.float32) + other.astype(jnp.float32)
-        moment_new = moment_decay * moment[j] + (1.0 - moment_decay) * gradient
-        second_new = square_decay * second[j] + (1.0 - square_decay) * gradient * gradient
-        divisor = second_new * lax.rsqrt(second_new) + adam_epsilon
-        adam_dir = moment_new * lax.rsqrt(divisor * divisor)
-        adam_sum = jnp.sum(adam_dir * adam_dir)
-        conditioned = dot(left_high, right) + dot(left_low, right)
+        applied, conditioned, squares = [], [], []
+        for n in range(2):
+            at = slice(n * half, (n + 1) * half)
+            gradient = first[:, at].astype(jnp.float32) + other[:, at].astype(jnp.float32)
+            applied.append(dot(left, gradient.astype(jnp.bfloat16)))
+            squares.append(adam_squares(n))
+        left_applied = jnp.concatenate(applied, axis=1).astype(jnp.bfloat16)
+        for n in range(2):
+            at = slice(n * half, (n + 1) * half)
+            conditioned.append(dot(left_applied, right[:, at]))
+            squares.append(adam_squares(2 + n))
+        conditioned = jnp.concatenate(conditioned, axis=1)
+        adam_sum = jnp.sum(squares[0] + squares[1] + squares[2] + squares[3])
         cond_sum = jnp.sum(conditioned * conditioned)
         graft = jnp.sqrt(adam_sum) / (jnp.sqrt(cond_sum) + norm_epsilon)
         held[j] = (conditioned * graft).astype(jnp.bfloat16).reshape(held.shape[1:])
@@ -172,7 +189,7 @@
         ],
         compiler_params=pltpu.CompilerParams(vmem_limit_bytes=24 * 2**20),
         cost_estimate=pl.CostEstimate(
-            flops=owned * 8 * width**3, bytes_accessed=11 * 2**20, transcendentals=0
+            flops=owned * 4 * width**3, bytes_accessed=11 * 2**20, transcendentals=0
         ),
         name="direction",
     )(arrived, root_left, root_right, moment, second)

time: 73.1 us -> 71.9 us (0.984)
  Pallas kernels: 19.5 us -> 18.2 us
    pallas_call x1, Pallas kernels: 4.55 us -> 3.33 us  [direction(): pl.pallas_call(direction_kernel, out_shape=pltpu.HBM((ranks, owned, share...]
where the time goes in v3:
time: 71.9 us; the launch traced here: 70.9 us
  blocking collectives  37.8 us (53%)
  Pallas kernels  18.2 us (25%)
  starting transfers between devices  9.66 us (13%)
  waiting for transfers between devices  4.58 us (6%)
    all_to_all x1, blocking collectives, exchange(): lax.all_to_all(chunks, every_axis, split_axis=0, concat_axis=0, tiled=Tru...  37.8 us
    all_to_all x1, starting transfers between devices, exchange(): lax.all_to_all(chunks, every_axis, split_axis=0, concat_axis=0, tiled=Tru...  9.57 us
    pallas_call x1, Pallas kernels, statistics(): pl.pallas_call(statistics_kernel, grid=(owned,), out_shape=[jax.ShapeDtyp...  7.85 us
    all_to_all x1, waiting for transfers between devices, exchange(): lax.all_to_all(chunks, every_axis, split_axis=0, concat_axis=0, tiled=Tru...  3.99 us
    pallas_call x1, Pallas kernels, preload(): pl.pallas_call(preload_kernel, out_shape=[pltpu.VMEM((near, *rest), halve...  3.55 us
    pallas_call x1, Pallas kernels, direction(): pl.pallas_call(direction_kernel, out_shape=pltpu.HBM((ranks, owned, share...  3.33 us
    pallas_call x1, Pallas kernels, pick(): pl.pallas_call(pick_kernel, out_shape=jax.ShapeDtypeStruct((near, *rest),...  1.58 us
  transfers between devices with their start and end apart: 2, of which 2 were waited for; matrix products, arithmetic and copies ran while one was open for 0% of the time, Pallas kernels for 16%

profile of v3, /device:TPU:0, one launch (start us, length us, event | category | flops | bytes accessed | tf_op | source)
XLA Modules:
  0.0 70.9 jit_solution(9900537208589451245)
XLA Ops:
  0.6 1.6 %pick.1 = bf16[2,64,16,512]{3,2,1,0:T(8,128)(2,1)S(1)} custom-call(bf16[2,2,64,16,512]{4,3,2,1,0:T(8,128)(2,1)} %bitcast.8), custom_call_target="tpu_custom_call" | custom-call | tf_op jit(solution)/shard_map/pick/pallas_call | solution.py:47
  2.2 0.1 collective-permute-start
  2.3 3.5 %preload.1 = (bf16[2,64,16,512]{3,2,1,0:T(8,128)(2,1)S(1)}, bf16[2,512,512]{2,1,0:T(8,128)(2,1)S(1)}, bf16[2,512,512]{2,1,0:T(8,128)(2,1)S(1)}, f32[2,512,512]{2,1,0:T(8,128)S(1)}, f32[2,512,512]{2,1,0:T(8,128)S(1)}) custom-call(bf16[2,2,64,16,512]{4,3,2,1,0:T(8,128)(2,1)} %bitcast.9, bf16[2,512,512]{2,1,0:T(8,128)(2,1)} %refs_0_.1, ...), custom_call_target="tpu_custom_call" | custom-call | bytes 10485760 | tf_op jit(solution)/shard_map/preload/pallas_call | solution.py:77
  5.9 0.6 collective-permute-done
  6.5 0.5 pair_add.1
  7.0 37.8 %all_to_all.10.arrived = bf16[64,2,16,512]{3,2,1,0:T(8,128)(2,1)S(1)} all-to-all(bf16[64,2,16,512]{3,2,1,0:T(8,128)(2,1)S(1)} %bitcast.5), channel_id=1, replica_groups={{95,0,1,2,3,4,5,6,7,8,9,10,11,12,13,14,15,16,17,18,19,20,21,22,23,24,25..., dimensions={0} | all-to-all | bytes 4194304 | tf_op jit(solution)/shard_map/all_to_all | solution.py:276
  44.8 3.3 %direction.1 = bf16[32,2,16,512]{3,2,1,0:T(8,128)(2,1)} custom-call(bf16[64,2,16,512]{3,2,1,0:T(8,128)(2,1)S(1)} %all_to_all.10.arrived, bf16[2,512,512]{2,1,0:T(8,128)(2,1)S(1)} %get-tuple-element.19.root_left, bf16[2,512,512]{2,1,0:T(8,128)(2,1)S(1)} %get-tuple-element.20.root_right, f32[2,512,512]{2,1,0:T(8,128)S(1)} %get-tuple-element.21.moment, ...), custom_call_target="tpu_custom_call" | custom-call | flops 1073741824 | bytes 11534336 | tf_op jit(solution)/shard_map/direction/pallas_call | solution.py:181
  48.1 9.6 %all-to-all-start.1 = ((bf16[32,2,16,512]{3,2,1,0:T(8,128)(2,1)}), bf16[32,2,16,512]{3,2,1,0:T(8,128)(2,1)S(1)}, u32[]{:S(2)}, u32[]{:S(2)}) async-start(bf16[32,2,16,512]{3,2,1,0:T(8,128)(2,1)} %direction.1), calls=%async_computation.1 | async-start | bytes 2097152 | tf_op jit(solution)/shard_map/all_to_all | solution.py:276
  57.7 7.9 %statistics.1 = (f32[2,512,512]{2,1,0:T(8,128)}, f32[2,512,512]{2,1,0:T(8,128)}, f32[2,512,512]{2,1,0:T(8,128)}, f32[2,512,512]{2,1,0:T(8,128)}) custom-call(bf16[64,2,16,512]{3,2,1,0:T(8,128)(2,1)S(1)} %all_to_all.10.arrived, f32[2,512,512]{2,1,0:T(8,128)} %stats_left.1, f32[2,512,512]{2,1,0:T(8,128)} %stats_right.1, f32[2,512,512]{2,1,0:T(8,128)} %moment.1, ...), custom_call_target="tpu_custom_call" | custom-call | flops 3221225472 | bytes 18874368 | tf_op jit(solution)/shard_map/statistics/pallas_call | solution.py:223
  65.6 4.0 %all-to-all-done.1.narrow = bf16[32,2,16,512]{3,2,1,0:T(8,128)(2,1)S(1)} async-done(((bf16[32,2,16,512]{3,2,1,0:T(8,128)(2,1)}), bf16[32,2,16,512]{3,2,1,0:T(8,128)(2,1)S(1)}, u32[]{:S(2)}, u32[]{:S(2)}) %all-to-all-start.1) | async-done | bytes 1048608 | tf_op jit(solution)/shard_map/all_to_all | solution.py:276
  69.6 1.4 %widen.1 = f32[32,2,16,512]{3,2,1,0:T(8,128)} custom-call(bf16[32,2,16,512]{3,2,1,0:T(8,128)(2,1)S(1)} %all-to-all-done.1.narrow), custom_call_target="tpu_custom_call" | custom-call | tf_op jit(solution)/shard_map/widen/pallas_call | solution.py:257
Async XLA Ops:
  2.2 4.2 %collective-permute-start = (bf16[2,64,16,512]{3,2,1,0:T(8,128)(2,1)S(1)}, bf16[2,64,16,512]{3,2,1,0:T(8,128)(2,1)S(1)}, u32[]{:S(2)}, u32[]{:S(2)}) collective-permute-start(bf16[2,64,16,512]{3,2,1,0:T(8,128)(2,1)S(1)} %pick.1), channel_id=1, source_target_pairs={{0,32},{32,0},{1,33},{33,1},{2,34},{34,2},{3,35},{35,3},{4,36},{36... | collective-permute-start | bytes 6291464 | tf_op jit(solution)/shard_map/ppermute | solution.py:289
  48.1 21.4 %all-to-all-start.1 = ((bf16[32,2,16,512]{3,2,1,0:T(8,128)(2,1)}), bf16[32,2,16,512]{3,2,1,0:T(8,128)(2,1)S(1)}, u32[]{:S(2)}, u32[]{:S(2)}) async-start(bf16[32,2,16,512]{3,2,1,0:T(8,128)(2,1)} %direction.1), calls=%async_computation.1 | async-start | bytes 2097152 | tf_op jit(solution)/shard_map/all_to_all | solution.py:276

commit v4 on v3

--- a/solution.py
+++ b/solution.py
@@ -25,17 +25,13 @@
     return jnp.dot(a, b, preferred_element_type=jnp.float32)
 
 
-def pick_kernel(halves, outgoing, sem):
+def pick_kernel(halves, *refs):
+    *outgoing, sem = refs
     core = lax.axis_index("core")
-    near, cuts = sem.shape
-    count = halves.shape[2] // cuts
-    copies = []
-    for n in range(near):
-        for c in range(cuts):
-            at = pl.ds(c * count, count)
-            copies.append(
-                pltpu.make_async_copy(halves.at[n, 1 - core, at], outgoing.at[n, at], sem.at[n, c])
-            )
+    copies = [
+        pltpu.make_async_copy(halves.at[n, 1 - core], target, sem.at[n])
+        for n, target in enumerate(outgoing)
+    ]
     for copy in copies:
         copy.start()
     for copy in copies:
@@ -46,10 +42,10 @@
     near, _, *rest = halves.shape
     return pl.pallas_call(
         pick_kernel,
-        out_shape=jax.ShapeDtypeStruct((near, *rest), halves.dtype),
+        out_shape=[jax.ShapeDtypeStruct(rest, halves.dtype)] * near,
         in_specs=[pl.BlockSpec(memory_space=pl.ANY)],
-        out_specs=pl.BlockSpec(memory_space=pl.ANY),
-        scratch_shapes=[pltpu.SemaphoreType.DMA((near, 4))],
+        out_specs=[pl.BlockSpec(memory_space=pl.ANY)] * near,
+        scratch_shapes=[pltpu.SemaphoreType.DMA((near,))],
         compiler_params=pltpu.CompilerParams(vmem_limit_bytes=4 * 2**20),
         name="pick",
     )(pltpu.with_memory_space_constraint(halves, pltpu.HBM))
@@ -87,32 +83,38 @@
     )(*(pltpu.with_memory_space_constraint(a, pltpu.HBM) for a in (halves, *arrays)))
 
 
-def pair_add_kernel(kept, swapped, total, *, turn):
+def pair_add_kernel(kept, *refs, turn):
+    *swapped, total = refs
     rows = 8
-    count = total.shape[0]
-
-    def add(source, size, target):
-        at = pl.ds(source, size)
-        both = kept[at].astype(jnp.float32) + swapped[at].astype(jnp.float32)
-        total[pl.ds(target, size)] = both.astype(total.dtype)
-
-    @pl.loop(0, count - rows, step=rows)
-    def _(i):
-        add(i, rows, i + turn)
-
-    add(count - rows, rows - turn, count - rows + turn)
-    add(count - turn, turn, 0)
+    count = swapped[0].shape[0]
+    last = len(swapped) - 1
+
+    def add(n, source, size):
+        both = kept[pl.ds(n * count + source, size)].astype(jnp.float32)
+        both = both + swapped[n][pl.ds(source, size)].astype(jnp.float32)
+        total[pl.ds(n * count + source + turn, size)] = both.astype(total.dtype)
+
+    for n in range(last + 1):
+        pl.loop(0, count - rows if n == last else count, step=rows)(
+            lambda i, n=n: add(n, i, rows)
+        )
+    add(last, count - rows, rows - turn)
+    ends = count - turn
+    both = kept[last * count + ends :].astype(jnp.float32)
+    both = both + swapped[last][ends:].astype(jnp.float32)
+    total[:turn] = both.astype(total.dtype)
 
 
 def pair_add(kept, swapped, turn):
+    inputs = [kept] + [pltpu.with_memory_space_constraint(a, pltpu.VMEM) for a in swapped]
     return pl.pallas_call(
         functools.partial(pair_add_kernel, turn=turn),
         out_shape=pltpu.VMEM(kept.shape, kept.dtype),
-        in_specs=[pl.BlockSpec(memory_space=pltpu.VMEM)] * 2,
+        in_specs=[pl.BlockSpec(memory_space=pltpu.VMEM)] * len(inputs),
         out_specs=pl.BlockSpec(memory_space=pltpu.VMEM),
         compiler_params=pltpu.CompilerParams(vmem_limit_bytes=8 * 2**20),
         name="pair_add",
-    )(kept, pltpu.with_memory_space_constraint(swapped, pltpu.VMEM))
+    )(*inputs)
 
 
 def pair_sums(arrived, j):
@@ -286,11 +288,11 @@
     _, row_share, block_width = pieces.shape
     block = (row_share, block_width)
     halves = pieces.reshape(near_count, 2, fsdp_count * owned_count, *block)
-    swapped = lax.ppermute(pick(halves), "core", [(0, 1), (1, 0)])
+    swapped = [lax.ppermute(part, "core", [(0, 1), (1, 0)]) for part in pick(halves)]
     kept, left_here, right_here, moment_here, second_here = preload(
         halves, root_left, root_right, moment, second
     )
-    pair_sum = pair_add(kept.reshape(-1, *block), swapped.reshape(-1, *block), owned_count)
+    pair_sum = pair_add(kept.reshape(-1, *block), swapped, owned_count)
 
     def rank(near, core, fsdp):
         return (near * 2 + core) * fsdp_count + fsdp

time: 71.9 us -> 71.9 us (level)
  transfers between devices with their start and end apart: 2 -> 3, of which waited for: 2 -> 2; matrix products, arithmetic and copies ran while one was open for 0% -> 0% of each run, Pallas kernels for 16% -> 16%
where the time goes in v4:
time: 71.9 us; the launch traced here: 70.9 us
  blocking collectives  37.8 us (53%)
  Pallas kernels  18.2 us (25%)
  starting transfers between devices  10.2 us (14%)
  waiting for transfers between devices  4.07 us (6%)
    all_to_all x1, blocking collectives, exchange(): lax.all_to_all(chunks, every_axis, split_axis=0, concat_axis=0, tiled=Tru...  37.8 us
    all_to_all x1, starting transfers between devices, exchange(): lax.all_to_all(chunks, every_axis, split_axis=0, concat_axis=0, tiled=Tru...  9.58 us
    pallas_call x1, Pallas kernels, statistics(): pl.pallas_call(statistics_kernel, grid=(owned,), out_shape=[jax.ShapeDtyp...  7.85 us
    all_to_all x1, waiting for transfers between devices, exchange(): lax.all_to_all(chunks, every_axis, split_axis=0, concat_axis=0, tiled=Tru...  3.97 us
    pallas_call x1, Pallas kernels, preload(): pl.pallas_call(preload_kernel, out_shape=[pltpu.VMEM((near, *rest), halve...  3.53 us
    pallas_call x1, Pallas kernels, direction(): pl.pallas_call(direction_kernel, out_shape=pltpu.HBM((ranks, owned, share...  3.33 us
    pallas_call x1, Pallas kernels, pick(): pl.pallas_call(pick_kernel, out_shape=[jax.ShapeDtypeStruct(rest, halves....  1.57 us
  transfers between devices with their start and end apart: 3, of which 2 were waited for; matrix products, arithmetic and copies ran while one was open for 0% of the time, Pallas kernels for 16%

profile of v4, /device:TPU:0, one launch (start us, length us, event | category | flops | bytes accessed | tf_op | source)
XLA Modules:
  0.0 70.9 jit_solution(6735426680227563661)
XLA Ops:
  0.6 1.6 %pick.1 = (bf16[64,16,512]{2,1,0:T(8,128)(2,1)S(1)}, bf16[64,16,512]{2,1,0:T(8,128)(2,1)S(1)}) custom-call(bf16[2,2,64,16,512]{4,3,2,1,0:T(8,128)(2,1)} %bitcast.6), custom_call_target="tpu_custom_call" | custom-call | tf_op jit(solution)/shard_map/pick/pallas_call | solution.py:43
  2.2 0.1 collective-permute-start
  2.3 0.5 collective-permute-start.1
  2.8 3.5 %preload.1 = (bf16[2,64,16,512]{3,2,1,0:T(8,128)(2,1)S(1)}, bf16[2,512,512]{2,1,0:T(8,128)(2,1)S(1)}, bf16[2,512,512]{2,1,0:T(8,128)(2,1)S(1)}, f32[2,512,512]{2,1,0:T(8,128)S(1)}, f32[2,512,512]{2,1,0:T(8,128)S(1)}) custom-call(bf16[2,2,64,16,512]{4,3,2,1,0:T(8,128)(2,1)} %bitcast.7, bf16[2,512,512]{2,1,0:T(8,128)(2,1)} %refs_0_.1, ...), custom_call_target="tpu_custom_call" | custom-call | bytes 10485760 | tf_op jit(solution)/shard_map/preload/pallas_call | solution.py:73
  6.3 0.0 collective-permute-done.refs_0_
  6.3 0.1 collective-permute-done.1.refs_1_
  6.4 0.5 pair_add.1
  7.0 37.8 %all_to_all.10.arrived = bf16[64,2,16,512]{3,2,1,0:T(8,128)(2,1)S(1)} all-to-all(bf16[64,2,16,512]{3,2,1,0:T(8,128)(2,1)S(1)} %bitcast.4), channel_id=1, replica_groups={{95,0,1,2,3,4,5,6,7,8,9,10,11,12,13,14,15,16,17,18,19,20,21,22,23,24,25..., dimensions={0} | all-to-all | bytes 4194304 | tf_op jit(solution)/shard_map/all_to_all | solution.py:278
  44.8 3.3 %direction.1 = bf16[32,2,16,512]{3,2,1,0:T(8,128)(2,1)} custom-call(bf16[64,2,16,512]{3,2,1,0:T(8,128)(2,1)S(1)} %all_to_all.10.arrived, bf16[2,512,512]{2,1,0:T(8,128)(2,1)S(1)} %get-tuple-element.23.root_left, bf16[2,512,512]{2,1,0:T(8,128)(2,1)S(1)} %get-tuple-element.24.root_right, f32[2,512,512]{2,1,0:T(8,128)S(1)} %get-tuple-element.25.moment, ...), custom_call_target="tpu_custom_call" | custom-call | flops 1073741824 | bytes 11534336 | tf_op jit(solution)/shard_map/direction/pallas_call | solution.py:183
  48.1 9.6 %all-to-all-start.1 = ((bf16[32,2,16,512]{3,2,1,0:T(8,128)(2,1)}), bf16[32,2,16,512]{3,2,1,0:T(8,128)(2,1)S(1)}, u32[]{:S(2)}, u32[]{:S(2)}) async-start(bf16[32,2,16,512]{3,2,1,0:T(8,128)(2,1)} %direction.1), calls=%async_computation.1 | async-start | bytes 2097152 | tf_op jit(solution)/shard_map/all_to_all | solution.py:278
  57.7 7.9 %statistics.1 = (f32[2,512,512]{2,1,0:T(8,128)}, f32[2,512,512]{2,1,0:T(8,128)}, f32[2,512,512]{2,1,0:T(8,128)}, f32[2,512,512]{2,1,0:T(8,128)}) custom-call(bf16[64,2,16,512]{3,2,1,0:T(8,128)(2,1)S(1)} %all_to_all.10.arrived, f32[2,512,512]{2,1,0:T(8,128)} %stats_left.1, f32[2,512,512]{2,1,0:T(8,128)} %stats_right.1, f32[2,512,512]{2,1,0:T(8,128)} %moment.1, ...), custom_call_target="tpu_custom_call" | custom-call | flops 3221225472 | bytes 18874368 | tf_op jit(solution)/shard_map/statistics/pallas_call | solution.py:225
  65.6 4.0 %all-to-all-done.1.narrow = bf16[32,2,16,512]{3,2,1,0:T(8,128)(2,1)S(1)} async-done(((bf16[32,2,16,512]{3,2,1,0:T(8,128)(2,1)}), bf16[32,2,16,512]{3,2,1,0:T(8,128)(2,1)S(1)}, u32[]{:S(2)}, u32[]{:S(2)}) %all-to-all-start.1) | async-done | bytes 1048608 | tf_op jit(solution)/shard_map/all_to_all | solution.py:278
  69.5 1.4 %widen.1 = f32[32,2,16,512]{3,2,1,0:T(8,128)} custom-call(bf16[32,2,16,512]{3,2,1,0:T(8,128)(2,1)S(1)} %all-to-all-done.1.narrow), custom_call_target="tpu_custom_call" | custom-call | tf_op jit(solution)/shard_map/widen/pallas_call | solution.py:259
Async XLA Ops:
  2.2 4.1 %collective-permute-start = (bf16[64,16,512]{2,1,0:T(8,128)(2,1)S(1)}, bf16[64,16,512]{2,1,0:T(8,128)(2,1)S(1)}, u32[]{:S(2)}, u32[]{:S(2)}) collective-permute-start(bf16[64,16,512]{2,1,0:T(8,128)(2,1)S(1)} %get-tuple-element.17), channel_id=1, source_target_pairs={{0,32},{32,0},{1,33},{33,1},{2,34},{34,2},{3,35},{35,3},{4,36},{36... | collective-permute-start | bytes 3145736 | tf_op jit(solution)/shard_map/ppermute | solution.py:291
  2.3 4.1 %collective-permute-start.1 = (bf16[64,16,512]{2,1,0:T(8,128)(2,1)S(1)}, bf16[64,16,512]{2,1,0:T(8,128)(2,1)S(1)}, u32[]{:S(2)}, u32[]{:S(2)}) collective-permute-start(bf16[64,16,512]{2,1,0:T(8,128)(2,1)S(1)} %get-tuple-element.18), channel_id=1, source_target_pairs={{0,32},{32,0},{1,33},{33,1},{2,34},{34,2},{3,35},{35,3},{4,36},{36... | collective-permute-start | bytes 3145736 | tf_op jit(solution)/shard_map/ppermute | solution.py:291
  48.1 21.4 %all-to-all-start.1 = ((bf16[32,2,16,512]{3,2,1,0:T(8,128)(2,1)}), bf16[32,2,16,512]{3,2,1,0:T(8,128)(2,1)S(1)}, u32[]{:S(2)}, u32[]{:S(2)}) async-start(bf16[32,2,16,512]{3,2,1,0:T(8,128)(2,1)} %direction.1), calls=%async_computation.1 | async-start | bytes 2097152 | tf_op jit(solution)/shard_map/all_to_all | solution.py:278

commit v5 on v4

--- a/solution.py
+++ b/solution.py
@@ -89,20 +89,16 @@
     count = swapped[0].shape[0]
     last = len(swapped) - 1
 
-    def add(n, source, size):
-        both = kept[pl.ds(n * count + source, size)].astype(jnp.float32)
-        both = both + swapped[n][pl.ds(source, size)].astype(jnp.float32)
-        total[pl.ds(n * count + source + turn, size)] = both.astype(total.dtype)
+    def add(n, source, size, target):
+        both = kept[pl.ds(n * count + source, size)] + swapped[n][pl.ds(source, size)]
+        total[pl.ds(target, size)] = both
 
     for n in range(last + 1):
-        pl.loop(0, count - rows if n == last else count, step=rows)(
-            lambda i, n=n: add(n, i, rows)
+        pl.loop(0, count - rows if n == last else count, step=rows, unroll=2 if n < last else 1)(
+            lambda i, n=n: add(n, i, rows, n * count + i + turn)
         )
-    add(last, count - rows, rows - turn)
-    ends = count - turn
-    both = kept[last * count + ends :].astype(jnp.float32)
-    both = both + swapped[last][ends:].astype(jnp.float32)
-    total[:turn] = both.astype(total.dtype)
+    add(last, count - rows, rows - turn, total.shape[0] - rows + turn)
+    add(last, count - turn, turn, 0)
 
 
 def pair_add(kept, swapped, turn):

time: 71.9 us -> 71.6 us (level)
  no operation moved by 1% of the time
where the time goes in v5:
time: 71.6 us; the launch traced here: 70.6 us
  blocking collectives  37.8 us (53%)
  Pallas kernels  17.9 us (25%)
  starting transfers between devices  10.2 us (14%)
  waiting for transfers between devices  4.08 us (6%)
    all_to_all x1, blocking collectives, exchange(): lax.all_to_all(chunks, every_axis, split_axis=0, concat_axis=0, tiled=Tru...  37.8 us
    all_to_all x1, starting transfers between devices, exchange(): lax.all_to_all(chunks, every_axis, split_axis=0, concat_axis=0, tiled=Tru...  9.59 us
    pallas_call x1, Pallas kernels, statistics(): pl.pallas_call(statistics_kernel, grid=(owned,), out_shape=[jax.ShapeDtyp...  7.85 us
    all_to_all x1, waiting for transfers between devices, exchange(): lax.all_to_all(chunks, every_axis, split_axis=0, concat_axis=0, tiled=Tru...  3.97 us
    pallas_call x1, Pallas kernels, preload(): pl.pallas_call(preload_kernel, out_shape=[pltpu.VMEM((near, *rest), halve...  3.53 us
    pallas_call x1, Pallas kernels, direction(): pl.pallas_call(direction_kernel, out_shape=pltpu.HBM((ranks, owned, share...  3.32 us
    pallas_call x1, Pallas kernels, pick(): pl.pallas_call(pick_kernel, out_shape=[jax.ShapeDtypeStruct(rest, halves....  1.57 us
  transfers between devices with their start and end apart: 3, of which 2 were waited for; matrix products, arithmetic and copies ran while one was open for 0% of the time, Pallas kernels for 16%

profile of v5, /device:TPU:0, one launch (start us, length us, event | category | flops | bytes accessed | tf_op | source)
XLA Modules:
  0.0 70.6 jit_solution(3424048107349230561)
XLA Ops:
  0.6 1.6 %pick.1 = (bf16[64,16,512]{2,1,0:T(8,128)(2,1)S(1)}, bf16[64,16,512]{2,1,0:T(8,128)(2,1)S(1)}) custom-call(bf16[2,2,64,16,512]{4,3,2,1,0:T(8,128)(2,1)} %bitcast.6), custom_call_target="tpu_custom_call" | custom-call | tf_op jit(solution)/shard_map/pick/pallas_call | solution.py:43
  2.2 0.1 collective-permute-start
  2.3 0.5 collective-permute-start.1
  2.8 3.5 %preload.1 = (bf16[2,64,16,512]{3,2,1,0:T(8,128)(2,1)S(1)}, bf16[2,512,512]{2,1,0:T(8,128)(2,1)S(1)}, bf16[2,512,512]{2,1,0:T(8,128)(2,1)S(1)}, f32[2,512,512]{2,1,0:T(8,128)S(1)}, f32[2,512,512]{2,1,0:T(8,128)S(1)}) custom-call(bf16[2,2,64,16,512]{4,3,2,1,0:T(8,128)(2,1)} %bitcast.7, bf16[2,512,512]{2,1,0:T(8,128)(2,1)} %refs_0_.1, ...), custom_call_target="tpu_custom_call" | custom-call | bytes 10485760 | tf_op jit(solution)/shard_map/preload/pallas_call | solution.py:73
  6.3 0.0 collective-permute-done.refs_0_
  6.3 0.1 collective-permute-done.1.refs_1_
  6.4 0.2 pair_add.1
  6.7 37.8 %all_to_all.10.arrived = bf16[64,2,16,512]{3,2,1,0:T(8,128)(2,1)S(1)} all-to-all(bf16[64,2,16,512]{3,2,1,0:T(8,128)(2,1)S(1)} %bitcast.4), channel_id=1, replica_groups={{95,0,1,2,3,4,5,6,7,8,9,10,11,12,13,14,15,16,17,18,19,20,21,22,23,24,25..., dimensions={0} | all-to-all | bytes 4194304 | tf_op jit(solution)/shard_map/all_to_all | solution.py:274
  44.5 3.3 %direction.1 = bf16[32,2,16,512]{3,2,1,0:T(8,128)(2,1)} custom-call(bf16[64,2,16,512]{3,2,1,0:T(8,128)(2,1)S(1)} %all_to_all.10.arrived, bf16[2,512,512]{2,1,0:T(8,128)(2,1)S(1)} %get-tuple-element.23.root_left, bf16[2,512,512]{2,1,0:T(8,128)(2,1)S(1)} %get-tuple-element.24.root_right, f32[2,512,512]{2,1,0:T(8,128)S(1)} %get-tuple-element.25.moment, ...), custom_call_target="tpu_custom_call" | custom-call | flops 1073741824 | bytes 11534336 | tf_op jit(solution)/shard_map/direction/pallas_call | solution.py:179
  47.8 9.6 %all-to-all-start.1 = ((bf16[32,2,16,512]{3,2,1,0:T(8,128)(2,1)}), bf16[32,2,16,512]{3,2,1,0:T(8,128)(2,1)S(1)}, u32[]{:S(2)}, u32[]{:S(2)}) async-start(bf16[32,2,16,512]{3,2,1,0:T(8,128)(2,1)} %direction.1), calls=%async_computation.1 | async-start | bytes 2097152 | tf_op jit(solution)/shard_map/all_to_all | solution.py:274
  57.4 7.9 %statistics.1 = (f32[2,512,512]{2,1,0:T(8,128)}, f32[2,512,512]{2,1,0:T(8,128)}, f32[2,512,512]{2,1,0:T(8,128)}, f32[2,512,512]{2,1,0:T(8,128)}) custom-call(bf16[64,2,16,512]{3,2,1,0:T(8,128)(2,1)S(1)} %all_to_all.10.arrived, f32[2,512,512]{2,1,0:T(8,128)} %stats_left.1, f32[2,512,512]{2,1,0:T(8,128)} %stats_right.1, f32[2,512,512]{2,1,0:T(8,128)} %moment.1, ...), custom_call_target="tpu_custom_call" | custom-call | flops 3221225472 | bytes 18874368 | tf_op jit(solution)/shard_map/statistics/pallas_call | solution.py:221
  65.3 4.0 %all-to-all-done.1.narrow = bf16[32,2,16,512]{3,2,1,0:T(8,128)(2,1)S(1)} async-done(((bf16[32,2,16,512]{3,2,1,0:T(8,128)(2,1)}), bf16[32,2,16,512]{3,2,1,0:T(8,128)(2,1)S(1)}, u32[]{:S(2)}, u32[]{:S(2)}) %all-to-all-start.1) | async-done | bytes 1048608 | tf_op jit(solution)/shard_map/all_to_all | solution.py:274
  69.2 1.4 %widen.1 = f32[32,2,16,512]{3,2,1,0:T(8,128)} custom-call(bf16[32,2,16,512]{3,2,1,0:T(8,128)(2,1)S(1)} %all-to-all-done.1.narrow), custom_call_target="tpu_custom_call" | custom-call | tf_op jit(solution)/shard_map/widen/pallas_call | solution.py:255
Async XLA Ops:
  2.2 4.1 %collective-permute-start = (bf16[64,16,512]{2,1,0:T(8,128)(2,1)S(1)}, bf16[64,16,512]{2,1,0:T(8,128)(2,1)S(1)}, u32[]{:S(2)}, u32[]{:S(2)}) collective-permute-start(bf16[64,16,512]{2,1,0:T(8,128)(2,1)S(1)} %get-tuple-element.17), channel_id=1, source_target_pairs={{0,32},{32,0},{1,33},{33,1},{2,34},{34,2},{3,35},{35,3},{4,36},{36... | collective-permute-start | bytes 3145736 | tf_op jit(solution)/shard_map/ppermute | solution.py:287
  2.3 4.1 %collective-permute-start.1 = (bf16[64,16,512]{2,1,0:T(8,128)(2,1)S(1)}, bf16[64,16,512]{2,1,0:T(8,128)(2,1)S(1)}, u32[]{:S(2)}, u32[]{:S(2)}) collective-permute-start(bf16[64,16,512]{2,1,0:T(8,128)(2,1)S(1)} %get-tuple-element.18), channel_id=1, source_target_pairs={{0,32},{32,0},{1,33},{33,1},{2,34},{34,2},{3,35},{35,3},{4,36},{36... | collective-permute-start | bytes 3145736 | tf_op jit(solution)/shard_map/ppermute | solution.py:287
  47.8 21.4 %all-to-all-start.1 = ((bf16[32,2,16,512]{3,2,1,0:T(8,128)(2,1)}), bf16[32,2,16,512]{3,2,1,0:T(8,128)(2,1)S(1)}, u32[]{:S(2)}, u32[]{:S(2)}) async-start(bf16[32,2,16,512]{3,2,1,0:T(8,128)(2,1)} %direction.1), calls=%async_computation.1 | async-start | bytes 2097152 | tf_op jit(solution)/shard_map/all_to_all | solution.py:274

commit v6 on v5

--- a/solution.py
+++ b/solution.py
@@ -126,7 +126,7 @@
 def direction_kernel(arrived, root_left, root_right, moment, second, step, held, sem):
     owned = root_left.shape[0]
     ranks = held.shape[1]
-    cuts = sem.shape[1] - 1
+    cuts = sem.shape[1]
     width = root_left.shape[-1]
     half, quarter = width // 2, width // 4
     copies = []
@@ -159,14 +159,12 @@
         adam_sum = jnp.sum(squares[0] + squares[1] + squares[2] + squares[3])
         cond_sum = jnp.sum(conditioned * conditioned)
         graft = jnp.sqrt(adam_sum) / (jnp.sqrt(cond_sum) + norm_epsilon)
-        held[j] = (conditioned * graft).astype(jnp.bfloat16).reshape(held.shape[1:])
-        edges = [c * (ranks // cuts) for c in range(cuts)] + [ranks - 1, ranks]
-        for c in range(cuts + 1):
-            start, size = edges[c], edges[c + 1] - edges[c]
-            target = (start + 1) % ranks
-            copy = pltpu.make_async_copy(
-                held.at[j, pl.ds(start, size)], step.at[pl.ds(target, size), j], sem.at[j, c]
-            )
+        scaled = (conditioned * graft).astype(jnp.bfloat16).reshape(held.shape[1:])
+        for rank in range(ranks):
+            held[j, ranks - 1 - rank] = scaled[rank]
+        for c in range(cuts):
+            at = pl.ds(c * (ranks // cuts), ranks // cuts)
+            copy = pltpu.make_async_copy(held.at[j, at], step.at[at, j], sem.at[j, c])
             copy.start()
             copies.append(copy)
     for copy in copies:
@@ -183,7 +181,7 @@
         out_specs=pl.BlockSpec(memory_space=pl.ANY),
         scratch_shapes=[
             pltpu.VMEM((owned, ranks, share, width), jnp.bfloat16),
-            pltpu.SemaphoreType.DMA((owned, 5)),
+            pltpu.SemaphoreType.DMA((owned, 4)),
         ],
         compiler_params=pltpu.CompilerParams(vmem_limit_bytes=24 * 2**20),
         cost_estimate=pl.CostEstimate(
@@ -239,11 +237,8 @@
     copies = []
     for c in range(cuts):
         at = pl.ds(c * size, size)
-        if c < cuts - 1:
-            held[at] = narrow[pl.ds(c * size + 1, size)].astype(jnp.float32)
-        else:
-            held[pl.ds(c * size, size - 1)] = narrow[pl.ds(c * size + 1, size - 1)].astype(jnp.float32)
-            held[ranks - 1] = narrow[0].astype(jnp.float32)
+        for rank in range(c * size, (c + 1) * size):
+            held[rank] = narrow[ranks - 1 - rank].astype(jnp.float32)
         copy = pltpu.make_async_copy(held.at[at], wide.at[at], sem.at[c])
         copy.start()
         copies.append(copy)
@@ -298,7 +293,7 @@
         for core in range(2)
     ]
     return_groups = [
-        last_first([rank(near, core, f) for f in range(fsdp_count)])
+        [rank(near, core, f) for f in reversed(range(fsdp_count))]
         for near in range(near_count)
         for core in range(2)
     ]

time: 71.6 us -> 71.3 us (level)
  no operation moved by 1% of the time
where the time goes in v6:
time: 71.3 us; the launch traced here: 71 us
  blocking collectives  37.8 us (53%)
  Pallas kernels  17.9 us (25%)
  starting transfers between devices  10.3 us (14%)
  waiting for transfers between devices  4.39 us (6%)
    all_to_all x1, blocking collectives, exchange(): lax.all_to_all(chunks, every_axis, split_axis=0, concat_axis=0, tiled=Tru...  37.8 us
    all_to_all x1, starting transfers between devices, exchange(): lax.all_to_all(chunks, every_axis, split_axis=0, concat_axis=0, tiled=Tru...  9.68 us
    pallas_call x1, Pallas kernels, statistics(): pl.pallas_call(statistics_kernel, grid=(owned,), out_shape=[jax.ShapeDtyp...  7.87 us
    all_to_all x1, waiting for transfers between devices, exchange(): lax.all_to_all(chunks, every_axis, split_axis=0, concat_axis=0, tiled=Tru...  4.29 us
    pallas_call x1, Pallas kernels, preload(): pl.pallas_call(preload_kernel, out_shape=[pltpu.VMEM((near, *rest), halve...  3.53 us
    pallas_call x1, Pallas kernels, direction(): pl.pallas_call(direction_kernel, out_shape=pltpu.HBM((ranks, owned, share...  3.31 us
    pallas_call x1, Pallas kernels, pick(): pl.pallas_call(pick_kernel, out_shape=[jax.ShapeDtypeStruct(rest, halves....  1.57 us
  transfers between devices with their start and end apart: 3, of which 2 were waited for; matrix products, arithmetic and copies ran while one was open for 0% of the time, Pallas kernels for 16%

profile of v6, /device:TPU:0, one launch (start us, length us, event | category | flops | bytes accessed | tf_op | source)
XLA Modules:
  0.0 71.0 jit_solution(12071911823249988539)
XLA Ops:
  0.6 1.6 %pick.1 = (bf16[64,16,512]{2,1,0:T(8,128)(2,1)S(1)}, bf16[64,16,512]{2,1,0:T(8,128)(2,1)S(1)}) custom-call(bf16[2,2,64,16,512]{4,3,2,1,0:T(8,128)(2,1)} %bitcast.6), custom_call_target="tpu_custom_call" | custom-call | tf_op jit(solution)/shard_map/pick/pallas_call | solution.py:43
  2.2 0.1 collective-permute-start
  2.3 0.5 collective-permute-start.1
  2.8 3.5 %preload.1 = (bf16[2,64,16,512]{3,2,1,0:T(8,128)(2,1)S(1)}, bf16[2,512,512]{2,1,0:T(8,128)(2,1)S(1)}, bf16[2,512,512]{2,1,0:T(8,128)(2,1)S(1)}, f32[2,512,512]{2,1,0:T(8,128)S(1)}, f32[2,512,512]{2,1,0:T(8,128)S(1)}) custom-call(bf16[2,2,64,16,512]{4,3,2,1,0:T(8,128)(2,1)} %bitcast.7, bf16[2,512,512]{2,1,0:T(8,128)(2,1)} %refs_0_.1, ...), custom_call_target="tpu_custom_call" | custom-call | bytes 10485760 | tf_op jit(solution)/shard_map/preload/pallas_call | solution.py:73
  6.3 0.0 collective-permute-done.refs_0_
  6.3 0.1 collective-permute-done.1.refs_1_
  6.4 0.2 pair_add.1
  6.7 37.8 %all_to_all.10.arrived = bf16[64,2,16,512]{3,2,1,0:T(8,128)(2,1)S(1)} all-to-all(bf16[64,2,16,512]{3,2,1,0:T(8,128)(2,1)S(1)} %bitcast.4), channel_id=1, replica_groups={{95,0,1,2,3,4,5,6,7,8,9,10,11,12,13,14,15,16,17,18,19,20,21,22,23,24,25..., dimensions={0} | all-to-all | bytes 4194304 | tf_op jit(solution)/shard_map/all_to_all | solution.py:269
  44.5 3.3 %direction.1 = bf16[32,2,16,512]{3,2,1,0:T(8,128)(2,1)} custom-call(bf16[64,2,16,512]{3,2,1,0:T(8,128)(2,1)S(1)} %all_to_all.10.arrived, bf16[2,512,512]{2,1,0:T(8,128)(2,1)S(1)} %get-tuple-element.23.root_left, bf16[2,512,512]{2,1,0:T(8,128)(2,1)S(1)} %get-tuple-element.24.root_right, f32[2,512,512]{2,1,0:T(8,128)S(1)} %get-tuple-element.25.moment, ...), custom_call_target="tpu_custom_call" | custom-call | flops 1073741824 | bytes 11534336 | tf_op jit(solution)/shard_map/direction/pallas_call | solution.py:177
  47.8 9.7 %all-to-all-start.1 = ((bf16[32,2,16,512]{3,2,1,0:T(8,128)(2,1)}), bf16[32,2,16,512]{3,2,1,0:T(8,128)(2,1)S(1)}, u32[]{:S(2)}, u32[]{:S(2)}) async-start(bf16[32,2,16,512]{3,2,1,0:T(8,128)(2,1)} %direction.1), calls=%async_computation.1 | async-start | bytes 2097152 | tf_op jit(solution)/shard_map/all_to_all | solution.py:269
  57.5 7.9 %statistics.1 = (f32[2,512,512]{2,1,0:T(8,128)}, f32[2,512,512]{2,1,0:T(8,128)}, f32[2,512,512]{2,1,0:T(8,128)}, f32[2,512,512]{2,1,0:T(8,128)}) custom-call(bf16[64,2,16,512]{3,2,1,0:T(8,128)(2,1)S(1)} %all_to_all.10.arrived, f32[2,512,512]{2,1,0:T(8,128)} %stats_left.1, f32[2,512,512]{2,1,0:T(8,128)} %stats_right.1, f32[2,512,512]{2,1,0:T(8,128)} %moment.1, ...), custom_call_target="tpu_custom_call" | custom-call | flops 3221225472 | bytes 18874368 | tf_op jit(solution)/shard_map/statistics/pallas_call | solution.py:219
  65.4 4.3 %all-to-all-done.1.narrow = bf16[32,2,16,512]{3,2,1,0:T(8,128)(2,1)S(1)} async-done(((bf16[32,2,16,512]{3,2,1,0:T(8,128)(2,1)}), bf16[32,2,16,512]{3,2,1,0:T(8,128)(2,1)S(1)}, u32[]{:S(2)}, u32[]{:S(2)}) %all-to-all-start.1) | async-done | bytes 1048608 | tf_op jit(solution)/shard_map/all_to_all | solution.py:269
  69.7 1.4 %widen.1 = f32[32,2,16,512]{3,2,1,0:T(8,128)} custom-call(bf16[32,2,16,512]{3,2,1,0:T(8,128)(2,1)S(1)} %all-to-all-done.1.narrow), custom_call_target="tpu_custom_call" | custom-call | tf_op jit(solution)/shard_map/widen/pallas_call | solution.py:250
Async XLA Ops:
  2.2 4.1 %collective-permute-start = (bf16[64,16,512]{2,1,0:T(8,128)(2,1)S(1)}, bf16[64,16,512]{2,1,0:T(8,128)(2,1)S(1)}, u32[]{:S(2)}, u32[]{:S(2)}) collective-permute-start(bf16[64,16,512]{2,1,0:T(8,128)(2,1)S(1)} %get-tuple-element.17), channel_id=1, source_target_pairs={{0,32},{32,0},{1,33},{33,1},{2,34},{34,2},{3,35},{35,3},{4,36},{36... | collective-permute-start | bytes 3145736 | tf_op jit(solution)/shard_map/ppermute | solution.py:282
  2.3 4.1 %collective-permute-start.1 = (bf16[64,16,512]{2,1,0:T(8,128)(2,1)S(1)}, bf16[64,16,512]{2,1,0:T(8,128)(2,1)S(1)}, u32[]{:S(2)}, u32[]{:S(2)}) collective-permute-start(bf16[64,16,512]{2,1,0:T(8,128)(2,1)S(1)} %get-tuple-element.18), channel_id=1, source_target_pairs={{0,32},{32,0},{1,33},{33,1},{2,34},{34,2},{3,35},{35,3},{4,36},{36... | collective-permute-start | bytes 3145736 | tf_op jit(solution)/shard_map/ppermute | solution.py:282
  47.8 21.8 %all-to-all-start.1 = ((bf16[32,2,16,512]{3,2,1,0:T(8,128)(2,1)}), bf16[32,2,16,512]{3,2,1,0:T(8,128)(2,1)S(1)}, u32[]{:S(2)}, u32[]{:S(2)}) async-start(bf16[32,2,16,512]{3,2,1,0:T(8,128)(2,1)} %direction.1), calls=%async_computation.1 | async-start | bytes 2097152 | tf_op jit(solution)/shard_map/all_to_all | solution.py:269
